TPU v7x, 512 devices: a whole 4x8x8 slice. The times are simulated.
512 devices in a mesh: tok: 32 (over y, x), kv: 16 (over z, core).
Axes of the slice: x: 4, y: 8, z: 8, core: 2. Of those that a mesh axis runs over, the one named last changes fastest.
Arguments:
- hidden_in: bfloat16 [32768, 1024], P(('tok', 'kv')), may hold values from -12 to 12
- qkv_weight: bfloat16 [1024, 3, 1024], P(None, None, 'kv'), may hold values from -1 to 1
- stretch_len: int32 [48], replicated, may hold values from 1 to 1024, 32768 in all
- out_weight: bfloat16 [1024, 1024], P('kv'), may hold values from -0.1875 to 0.1875
- ln1_gain: float32 [1024], replicated, may hold values from 0.5 to 1.5
- ln1_bias: float32 [1024], replicated, may hold values from -3 to 3
- up_weight: bfloat16 [1024, 4096], P(None, 'kv'), may hold values from -0.1875 to 0.1875
- down_weight: bfloat16 [4096, 1024], P('kv'), may hold values from -0.09375 to 0.09375
- ln2_gain: float32 [1024], replicated, may hold values from 0.5 to 1.5
- ln2_bias: float32 [1024], replicated, may hold values from -3 to 3
- dec_query: bfloat16 [1024, 1024], P(('tok', 'kv')), may hold values from -12 to 12
- kv_cache: bfloat16 [2, 32, 96, 128, 1024], P(None, 'tok', 'kv'), may hold values from -12 to 12
- piece_req: int32 [32, 96], P('tok', 'kv'), may hold values from 0 to 31, as said below
- piece_used: int32 [32, 96], P('tok', 'kv'), may hold values from 0 to 128, as said below
Outputs:
- prefill_out: bfloat16 [32768, 1024], P(('tok', 'kv'))
- dec_out: bfloat16 [1024, 1024], P(('tok', 'kv'))
Inputs may be any that keep to these rules, and one draw needn't show every extreme that they name: `piece_req`: every request of an index of tok owns at least one piece of that index with a nonzero count. `piece_used`: slots with a count of 0 hold no tokens.
All inputs are finite; a program needn't handle non-finite values.
Results may differ from a plain program's by a relative error of at most 0.017.
Values may be sent and summed in bfloat16 or wider, within the bound.
A program may use at most 64 MiB of HBM per device.

v0:
```python
import math

import jax
import jax.numpy as jnp
from jax import lax
from jax.sharding import PartitionSpec as P

H = 16
HD = 64
WIN = 512
PLEN = 128


NEG_FILL = -1e30
LN_EPS = 1e-05


def extended(value, sides, width):
    for axis, dim in sides:
        count, length = (lax.axis_size(axis), value.shape[dim])
        up = [(i, (i + 1) % count) for i in range(count - 1)]
        down = [(j, i) for i, j in up]
        last = lax.slice_in_dim(value, length - width, length, axis=dim)
        leading = lax.slice_in_dim(value, 0, width, axis=dim)
        before = lax.ppermute(last, axis, up)
        after = lax.ppermute(leading, axis, down)
        value = jnp.concatenate([before, value, after], axis=dim)
    return value


def merged(value, axis, join):
    pieces = jax.tree.map(lambda part: lax.all_gather(part, axis), value)
    head = jax.tree.map(lambda part: part[0], pieces)
    tail = jax.tree.map(lambda part: part[1:], pieces)
    subtotal, _ = lax.scan(lambda subtotal, section: (join(subtotal, section), None), head, tail)
    return subtotal


def segment_ids(row_ids, stretch_len):
    stretch_ends = jnp.cumsum(stretch_len)
    return jnp.sum((row_ids[:, None] >= stretch_ends[None, :]).astype(jnp.int32), axis=1)


def layer_norm(values, gain, bias):
    center = values - jnp.mean(values, axis=1, keepdims=True)
    spread = jnp.mean(center * center, axis=1, keepdims=True)
    return center * lax.rsqrt(spread + LN_EPS) * gain + bias


def merge_partials(earlier, later):
    highest = jnp.maximum(earlier[0], later[0])
    left_factor = jnp.exp(earlier[0] - highest)
    right_factor = jnp.exp(later[0] - highest)
    totals = earlier[1] * left_factor + later[1] * right_factor
    weighted = earlier[2] * left_factor[..., None] + later[2] * right_factor[..., None]
    return (highest, totals, weighted)


def row_folder(source, shard_rows):
    return jnp.dot(source, shard_rows, preferred_element_type=jnp.float32)


def body(
    hidden_in,
    qkv_weight,
    stretch_len,
    out_weight,
    ln1_gain,
    ln1_bias,
    up_weight,
    down_weight,
    ln2_gain,
    ln2_bias,
    dec_query,
    kv_cache,
    piece_req,
    piece_used,
):
    inv_scale = 1.0 / math.sqrt(HD)
    reach = WIN // 2
    local_width = qkv_weight.shape[2]
    head_count = local_width // HD
    flat_weight = qkv_weight.reshape(qkv_weight.shape[0], 3 * local_width)
    qkv_rows = jnp.dot(
        lax.all_gather(hidden_in, "kv", axis=0, tiled=True),
        flat_weight,
        preferred_element_type=jnp.float32,
    ).astype(jnp.bfloat16)
    row_count = qkv_rows.shape[0]
    query_rows = qkv_rows[:, :local_width]
    keyval_rows = qkv_rows[:, local_width:]
    padded = extended(keyval_rows, (("tok", 0),), reach)
    first_row = lax.axis_index("tok") * row_count
    total_rows = row_count * lax.axis_size("tok")
    qblock = min(512, row_count)
    span = qblock + 2 * reach
    block_count = row_count // qblock

    def attend(block_index):
        start = block_index * qblock
        query_ids = first_row + start + jnp.arange(qblock, dtype=jnp.int32)
        key_ids = first_row + start - reach + jnp.arange(span, dtype=jnp.int32)
        query_seg = segment_ids(query_ids, stretch_len)
        inside = (key_ids >= 0) & (key_ids < total_rows)
        key_seg = jnp.where(inside, segment_ids(key_ids, stretch_len), -1)
        allowed = (key_seg[None, :] == query_seg[:, None]) & (
            jnp.abs(key_ids[None, :] - query_ids[:, None]) <= reach
        )
        queries = lax.dynamic_slice_in_dim(query_rows, start, qblock, 0).reshape(
            qblock, head_count, HD
        )
        both = lax.dynamic_slice_in_dim(padded, start, span, 0)
        key_rows = both[:, :local_width].reshape(span, head_count, HD)
        value_rows = both[:, local_width:].reshape(span, head_count, HD)
        scores = (
            jnp.einsum("ihd,jhd->hij", queries, key_rows, preferred_element_type=jnp.float32)
            * inv_scale
        )
        scores = jnp.where(allowed[None], scores, NEG_FILL)
        row_max = jnp.max(scores, axis=2, keepdims=True)
        weights = jnp.where(allowed[None], jnp.exp(scores - row_max), 0.0)
        totals = jnp.sum(weights, axis=2)
        summed = jnp.einsum(
            "hij,jhd->ihd",
            weights.astype(jnp.bfloat16),
            value_rows,
            preferred_element_type=jnp.float32,
        )
        return (
            (summed / jnp.transpose(totals)[:, :, None])
            .astype(jnp.bfloat16)
            .reshape(qblock, local_width)
        )

    attention = lax.map(attend, jnp.arange(block_count, dtype=jnp.int32)).reshape(
        row_count, local_width
    )
    token_major = lax.all_to_all(attention, "kv", split_axis=0, concat_axis=1, tiled=True)
    projected = row_folder(token_major, lax.all_gather(out_weight, "kv", axis=0, tiled=True))
    normed = layer_norm(hidden_in.astype(jnp.float32) + projected, ln1_gain, ln1_bias).astype(
        jnp.bfloat16
    )
    units = jax.nn.gelu(
        jnp.dot(
            lax.all_gather(normed, "kv", axis=0, tiled=True),
            up_weight,
            preferred_element_type=jnp.float32,
        ),
        approximate=False,
    ).astype(jnp.bfloat16)
    ffn = lax.psum_scatter(
        jnp.dot(units, down_weight, preferred_element_type=jnp.float32).astype(jnp.bfloat16),
        "kv",
        scatter_dimension=0,
        tiled=True,
    ).astype(jnp.float32)
    prefill_out = layer_norm(normed.astype(jnp.float32) + ffn, ln2_gain, ln2_bias).astype(
        jnp.bfloat16
    )
    group_queries = lax.all_gather(dec_query, "kv", axis=0, tiled=True)
    request_count = group_queries.shape[0]
    owners = piece_req[0]
    filled = piece_used[0]
    slot_count = owners.shape[0]
    request_ids = jnp.arange(request_count, dtype=jnp.int32)
    selector = (owners[:, None] == request_ids[None, :]).astype(jnp.bfloat16)
    chosen = jnp.dot(selector, group_queries, preferred_element_type=jnp.float32).astype(
        jnp.bfloat16
    )
    chosen = chosen.reshape(slot_count, H, HD)
    cache_keys = kv_cache[0, 0].reshape(slot_count, PLEN, H, HD)
    cache_values = kv_cache[1, 0].reshape(slot_count, PLEN, H, HD)
    piece_scores = (
        jnp.einsum("phd,pthd->pht", chosen, cache_keys, preferred_element_type=jnp.float32)
        * inv_scale
    )
    active = jnp.arange(PLEN, dtype=jnp.int32)[None, :] < filled[:, None]
    piece_scores = jnp.where(active[:, None, :], piece_scores, NEG_FILL)
    piece_max = jnp.max(piece_scores, axis=2)
    piece_weights = jnp.where(
        active[:, None, :], jnp.exp(piece_scores - piece_max[:, :, None]), 0.0
    )
    piece_totals = jnp.sum(piece_weights, axis=2)
    partial_value = jnp.einsum(
        "pht,pthd->phd",
        piece_weights.astype(jnp.bfloat16),
        cache_values,
        preferred_element_type=jnp.float32,
    )
    member = (owners[None, :] == request_ids[:, None]) & (filled[None, :] > 0)
    highest = jnp.max(jnp.where(member[:, :, None], piece_max[None], NEG_FILL), axis=1)
    factor = jnp.where(member[:, :, None], jnp.exp(piece_max[None] - highest[:, None, :]), 0.0)
    denom = jnp.sum(factor * piece_totals[None], axis=1)
    weighted = jnp.einsum("rph,phd->rhd", factor, partial_value)
    own_requests = dec_query.shape[0]
    joined = merged((highest, denom, weighted), "kv", merge_partials)
    begin = lax.axis_index("kv") * own_requests
    final_denom = lax.dynamic_slice_in_dim(joined[1], begin, own_requests, 0)
    final_weighted = lax.dynamic_slice_in_dim(joined[2], begin, own_requests, 0)
    dec_out = (
        (final_weighted / final_denom[:, :, None])
        .astype(jnp.bfloat16)
        .reshape(own_requests, H * HD)
    )
    return (prefill_out, dec_out)


def solution(mesh):
    placed = (
        P(("tok", "kv"), None),
        P(None, None, "kv"),
        P(),
        P("kv", None),
        P(),
        P(),
        P(None, "kv"),
        P("kv", None),
        P(),
        P(),
        P(("tok", "kv"), None),
        P(None, "tok", "kv", None, None),
        P("tok", "kv"),
        P("tok", "kv"),
    )
    return jax.shard_map(
        body,
        mesh=mesh,
        in_specs=placed,
        out_specs=(P(("tok", "kv"), None), P(("tok", "kv"), None)),
        check_vma=False,
    )
```

profile of v0, /device:TPU:1, one launch (start us, length us, event | category | flops | bytes accessed | tf_op | source)
XLA Modules:
  0.0 269.1 jit_solution(17714774776569042649)
XLA Ops:
  8.7 3.5 %fusion.114 = (bf16[1,1,6,128,1024]{4,3,2,1,0:T(8,128)(2,1)S(1)}, bf16[1,1,6,128,1024]{4,3,2,1,0:T(8,128)(2,1)}) fusion(bf16[2,1,6,128,1024]{4,3,2,1,0:T(8,128)(2,1)} %param.29), kind=kLoop, calls=%fused_computation.162 | loop fusion | bytes 6291456 | tf_op jit(solution)/shard_map/slice | solution.py:172
  12.2 2.6 copy.71
  14.8 24.7 %all-gather.3 = bf16[16,2,1024]{2,1,0:T(2,128)(2,1)S(1)} all-gather(bf16[1,2,1024]{2,1,0:T(2,128)(2,1)S(1)} %bitcast.103), channel_id=1, replica_groups=mesh['tok'=32,'kv'=16] {'kv'}, dimensions={0}, use_global_device_ids=true | all-gather | bytes 69632 | tf_op jit(solution)/shard_map/all_gather | solution.py:160
  39.9 1.9 fusion.119
  42.0 1.6 copy.72
  43.9 2.3 fusion.70
  46.3 13.2 %all-gather.11.cloned.1.call-done = bf16[1024,1024]{1,0:T(8,128)(2,1)} async-done(((bf16[64,1024]{1,0:T(8,128)(2,1)}), bf16[1024,1024]{1,0:T(8,128)(2,1)}) %all-gather.11.cloned.1.call-update) | async-done | bytes 2097168 | tf_op jit(solution)/shard_map/all_gather | solution.py:85
  59.4 2.4 convolution_convert_fusion.1
  61.9 2.8 %collective-permute-start = (bf16[256,128]{0,1:T(8,128)(2,1)S(1)}, bf16[256,128]{0,1:T(8,128)(2,1)S(1)}, u32[]{:S(2)}, u32[]{:S(2)}) collective-permute-start(bf16[256,128]{0,1:T(8,128)(2,1)S(1)} %get-tuple-element.226), channel_id=1, source_target_pairs={{0,16},{16,32},{32,48},{48,64},{64,80},{80,96},{96,112},{112,128},... | collective-permute-start | bytes 196616 | tf_op jit(solution)/shard_map/ppermute | solution.py:25
  64.7 1.3 collective-permute-start.1
  66.0 1.1 convolution_bitcast_fusion.1
  67.5 2.2 collective-permute-done.1
  69.8 9.1 %while.26 = (s32[]{:T(128)}, bf16[2,512,64]{1,2,0:T(8,128)(2,1)S(1)}, s32[2]{0:T(128)S(1)}, bf16[1536,128]{0,1:T(8,128)(2,1)S(1)}, s32[]{:T(128)}, /*index=5*/s3...) while((s32[]{:T(128)}, ...), condition=%wide.region_6.7_spmd, body=%wide.region_1.6_spmd.sunk | while | flops 149188608 | bytes 6759068 | solution.py:135
  72.2 1.1 fusion.141
  73.3 1.0 fusion.142
  76.8 1.1 fusion.141
  77.9 1.0 fusion.142
  79.6 15.0 %all_to_all.19 = bf16[16,2,2048]{2,1,0:T(2,128)(2,1)S(1)} all-to-all(bf16[16,2,2048]{2,1,0:T(2,128)(2,1)S(1)} %reshape.209), channel_id=1, replica_groups=mesh['tok'=32,'kv'=16] {'kv'}, dimensions={0} | all-to-all | bytes 262144 | tf_op jit(solution)/shard_map/all_to_all | solution.py:138
  94.8 8.2 %all-gather.13.cloned.1.call-done = bf16[1024,1024]{1,0:T(8,128)(2,1)} async-done(((bf16[64,1024]{1,0:T(8,128)(2,1)}), bf16[1024,1024]{1,0:T(8,128)(2,1)}) %all-gather.13.cloned.1.call-update) | async-done | bytes 2097168 | tf_op jit(solution)/shard_map/all_gather | solution.py:139
  103.0 2.2 fusion.116
  106.5 16.8 %all-gather.5 = f32[16,32,16]{1,2,0:T(8,128)S(1)} all-gather(f32[1,32,16]{1,2,0:T(8,128)S(1)} %bitcast.102), channel_id=3, replica_groups=mesh['tok'=32,'kv'=16] {'kv'}, dimensions={0}, use_global_device_ids=true | all-gather | bytes 34816 | tf_op jit(solution)/shard_map/all_gather | solution.py:32
  123.2 15.1 %all-gather.4 = f32[16,32,16]{1,2,0:T(8,128)S(1)} all-gather(f32[1,32,16]{1,2,0:T(8,128)S(1)} %bitcast.99), channel_id=2, replica_groups=mesh['tok'=32,'kv'=16] {'kv'}, dimensions={0}, use_global_device_ids=true | all-gather | bytes 34816 | tf_op jit(solution)/shard_map/all_gather | solution.py:32
  138.3 11.1 %all-gather.17.cloned.1.call-done = f32[512,16,64]{2,0,1:T(8,128)} async-done(((f32[32,16,64]{2,0,1:T(8,128)}), f32[512,16,64]{2,0,1:T(8,128)}) %all-gather.17.cloned.1.call-update) | async-done | bytes 2097168 | tf_op jit(solution)/shard_map/all_gather | solution.py:32
  150.6 4.3 %slice.81 = f32[480,16,64]{2,0,1:T(8,128)} slice(f32[512,16,64]{2,0,1:T(8,128)} %all-gather.17.cloned.1.call-done), slice={[32:512], [0:16], [0:64]} | slice | bytes 3932160 | tf_op jit(solution)/shard_map/slice | solution.py:34
  154.9 38.6 %all-gather.15.cloned.1.call-done = bf16[1024,1024]{1,0:T(8,128)(2,1)} async-done(((bf16[64,1024]{1,0:T(8,128)(2,1)}), bf16[1024,1024]{1,0:T(8,128)(2,1)}) %all-gather.15.cloned.1.call-update) | async-done | bytes 2097168 | tf_op jit(solution)/shard_map/all_gather | solution.py:145
  193.5 7.2 %convolution_convert_fusion = bf16[1024,1024]{1,0:T(8,128)(2,1)} fusion(bf16[256,1024]{1,0:T(8,128)(2,1)S(1)} %copy-done, bf16[1024,1024]{1,0:T(8,128)(2,1)} %all-gather.15.cloned.1.call-done, bf16[1024,256]{1,0:T(8,128)(2,1)S(1)} %copy-done.10), kind=kOutput, calls=%fused_computation.38 | convolution fusion | flops 1091829760 | bytes 5242880 | tf_op jit(solution)/shard_map/dot_general | solution.py:152
  201.7 22.1 %while.27 = (s32[]{:T(128)}, f32[32,16]{0,1:T(8,128)S(1)}, f32[32,16]{0,1:T(8,128)S(1)}, f32[32,16,64]{2,1,0:T(8,128)S(1)}, f32[15,32,16]{1,2,0:T(8,128)S(1)}, /...) while((s32[]{:T(128)}, f32[32,16]{0,1:T(8,128)S(1)}, f32[32,16]{0,1:T(8,128)S(1)}, ...), condition=%wide.region_17.18_spmd, body=%wide.region_16.17_spmd.sunk | while | flops 101378 | bytes 684125 | solution.py:35
  212.2 1.0 constant_dynamic-slice_fusion.3
  224.7 33.8 %reduce-scatter.2.cloned.1.call-done = bf16[64,1024]{1,0:T(8,128)(2,1)} async-done(((bf16[1024,1024]{1,0:T(8,128)(2,1)}), bf16[64,1024]{1,0:T(8,128)(2,1)}) %reduce-scatter.2.cloned.1.call-update) | async-done | bytes 131088 | tf_op jit(solution)/shard_map/reduce_scatter | solution.py:151
  258.5 1.1 fusion.67
  259.7 1.2 multiply_reduce_fusion
  260.9 1.7 add_convert_fusion
  (169 shorter events, 32.1 us)
Async XLA Ops:
  7.2 186.4 %copy-start = (bf16[256,1024]{1,0:T(8,128)(2,1)S(1)}, bf16[256,1024]{1,0:T(8,128)(2,1)}, u32[]{:S(2)}) copy-start(bf16[256,1024]{1,0:T(8,128)(2,1)} %param.25) | copy-start | bytes 1572868
  7.2 52.2 %all-gather.11.cloned.1.call-start = ((), (), s32[]{:S(2)}) async-start(), calls=%async_computation.2 | async-start | bytes 2228224 | tf_op jit(solution)/shard_map/all_gather | solution.py:85
  7.9 95.1 %all-gather.13.cloned.1.call-start = ((), (), s32[]{:S(2)}) async-start(), calls=%async_computation.3 | async-start | bytes 2228224 | tf_op jit(solution)/shard_map/all_gather | solution.py:139
  8.7 140.8 %all-gather.17.cloned.1.call-start = ((), (), s32[]{:S(2)}) async-start(), calls=%async_computation.6 | async-start | bytes 4456448 | tf_op jit(solution)/shard_map/all_gather | solution.py:32
  12.2 2.6 copy-start.8
  12.2 27.3 %copy-start.9 = (s32[1,6]{1,0:T(1,128)S(1)}, s32[1,6]{1,0:T(1,128)}, u32[]{:S(2)}) copy-start(s32[1,6]{1,0:T(1,128)} %param.30) | copy-start | bytes 76
  12.2 27.6 %copy-start.12 = (s32[1,6]{1,0:T(1,128)S(1)}, s32[1,6]{1,0:T(1,128)}, u32[]{:S(2)}) copy-start(s32[1,6]{1,0:T(1,128)} %param.31) | copy-start | bytes 76
  42.0 17.4 %copy-start.11 = (bf16[1024,3,64]{0,2,1:T(8,128)(2,1)S(1)}, bf16[1024,3,64]{0,2,1:T(8,128)(2,1)}, u32[]{:S(2)}) copy-start(bf16[1024,3,64]{0,2,1:T(8,128)(2,1)} %param.19) | copy-start | bytes 1179652
  59.4 7.8 %copy-start.13 = (s32[48]{0:T(128)S(1)}, s32[48]{0:T(128)}, u32[]{:S(2)}) copy-start(s32[48]{0:T(128)} %param.20) | copy-start | bytes 580
  61.9 5.6 %collective-permute-start = (bf16[256,128]{0,1:T(8,128)(2,1)S(1)}, bf16[256,128]{0,1:T(8,128)(2,1)S(1)}, u32[]{:S(2)}, u32[]{:S(2)}) collective-permute-start(bf16[256,128]{0,1:T(8,128)(2,1)S(1)} %get-tuple-element.226), channel_id=1, source_target_pairs={{0,16},{16,32},{32,48},{48,64},{64,80},{80,96},{96,112},{112,128},... | collective-permute-start | bytes 196616 | tf_op jit(solution)/shard_map/ppermute | solution.py:25
  64.7 5.0 %collective-permute-start.1 = (bf16[256,128]{0,1:T(8,128)(2,1)S(1)}, bf16[256,128]{0,1:T(8,128)(2,1)S(1)}, u32[]{:S(2)}, u32[]{:S(2)}) collective-permute-start(bf16[256,128]{0,1:T(8,128)(2,1)S(1)} %get-tuple-element.227), channel_id=1, source_target_pairs={{16,0},{32,16},{48,32},{64,48},{80,64},{96,80},{112,96},{128,112},... | collective-permute-start | bytes 196616 | tf_op jit(solution)/shard_map/ppermute | solution.py:26
  67.2 126.4 %all-gather.15.cloned.1.call-start = ((), (), s32[]{:S(2)}) async-start(), calls=%async_computation.4 | async-start | bytes 2228224 | tf_op jit(solution)/shard_map/all_gather | solution.py:145
  78.9 24.1 %copy-start.1 = (bf16[64,1024]{1,0:T(8,128)(2,1)S(1)}, bf16[64,1024]{1,0:T(8,128)(2,1)}, u32[]{:S(2)}) copy-start(bf16[64,1024]{1,0:T(8,128)(2,1)} %param.18) | copy-start | bytes 393220
  79.4 26.0 %copy-start.4 = (f32[1024]{0:T(1024)S(1)}, f32[1024]{0:T(1024)}, u32[]{:S(2)}) copy-start(f32[1024]{0:T(1024)} %param.23) | copy-start | bytes 12292
  79.4 26.0 %copy-start.5 = (f32[1024]{0:T(1024)S(1)}, f32[1024]{0:T(1024)}, u32[]{:S(2)}) copy-start(f32[1024]{0:T(1024)} %param.22) | copy-start | bytes 12292
  106.2 152.3 %reduce-scatter.2.cloned.1.call-start = ((), (), s32[]{:S(2)}) async-start(), calls=%async_computation.5 | async-start | bytes 2228224 | tf_op jit(solution)/shard_map/reduce_scatter | solution.py:151
  123.2 31.7 %copy-start.2 = (f32[16,32,16]{1,2,0:T(8,128)}, f32[16,32,16]{1,2,0:T(8,128)S(1)}, u32[]{:S(2)}) copy-start(f32[16,32,16]{1,2,0:T(8,128)S(1)} %all-gather.5) | copy-start | bytes 98308
  138.3 16.6 %copy-start.3 = (f32[16,32,16]{1,2,0:T(8,128)}, f32[16,32,16]{1,2,0:T(8,128)S(1)}, u32[]{:S(2)}) copy-start(f32[16,32,16]{1,2,0:T(8,128)S(1)} %all-gather.4) | copy-start | bytes 98308
  150.6 42.9 %copy-start.10 = (bf16[1024,256]{1,0:T(8,128)(2,1)S(1)}, bf16[1024,256]{1,0:T(8,128)(2,1)}, u32[]{:S(2)}) copy-start(bf16[1024,256]{1,0:T(8,128)(2,1)} %param.24) | copy-start | bytes 1572868
  200.7 0.9 slice-start
  200.7 1.0 slice-start.1
  201.7 59.2 %copy-start.6 = (f32[1024]{0:T(1024)S(1)}, f32[1024]{0:T(1024)}, u32[]{:S(2)}) copy-start(f32[1024]{0:T(1024)} %param.27) | copy-start | bytes 12292
  201.7 59.2 %copy-start.7 = (f32[1024]{0:T(1024)S(1)}, f32[1024]{0:T(1024)}, u32[]{:S(2)}) copy-start(f32[1024]{0:T(1024)} %param.26) | copy-start | bytes 12292
Sparse Core Ops, SparseCore 0:
  10.1 49.2 all-gather.10
  61.5 41.3 all-gather.12
  105.1 44.2 all-gather.16
  152.0 41.4 all-gather.14
  200.9 57.5 reduce-scatter.1
where the time goes:
time: 272 us; the launch traced here: 269 us
  waiting for transfers between devices  109 us (40%)
  blocking collectives  71.5 us (26%)
  local copies, waits for them, and re-layouts  34.2 us (13%)
  matrix products  21.3 us (8%)
  between operations  14.1 us (5%)
  other arithmetic  13.3 us (5%)
  starting transfers between devices  4.3 us (2%)
    all_gather x1, waiting for transfers between devices, body(): lax.all_gather(normed, 'kv', axis=0, tiled=True)  38.6 us
    reduce_scatter x1, waiting for transfers between devices, body(): lax.psum_scatter(jnp.dot(units, down_weight, preferred_element_type=jnp.f...  33.8 us
    all_gather x2, blocking collectives, merged(): pieces = jax.tree.map(lambda part: lax.all_gather(part, axis), value)  31.8 us
    all_gather x1, blocking collectives, body(): group_queries = lax.all_gather(dec_query, 'kv', axis=0, tiled=True)  24.7 us
    all_to_all x1, blocking collectives, body(): lax.all_to_all(attention, 'kv', split_axis=0, concat_axis=1, tiled=True)  15 us
    dynamic_slice x15, local copies, waits for them, and re-layouts, merged(): lax.scan(lambda subtotal, section: (join(subtotal, section), None), head,...  14.6 us
    all_gather x1, waiting for transfers between devices, body(): lax.all_gather(hidden_in, 'kv', axis=0, tiled=True)  13.2 us
    all_gather x1, waiting for transfers between devices, merged(): pieces = jax.tree.map(lambda part: lax.all_gather(part, axis), value)  11.1 us
  transfers between devices with their start and end apart: 7, of which 6 were waited for; matrix products, arithmetic and copies ran while one was open for 21% of the time, Pallas kernels for 0%

commit v1 on v0

v1 whole, which is shorter than its diff:
```python
import functools
import math

import jax
import jax.numpy as jnp
from jax import lax
from jax.experimental import pallas as pl
from jax.experimental.pallas import tpu as pltpu
from jax.sharding import PartitionSpec as P

MESH = pl.DeviceIdType.MESH
F32 = jnp.float32
BF16 = jnp.bfloat16
D = 1024
NZ = 8
NK = 16
NX = 4
NY = 8
NT = NX * NY
NSEG = 48
NPIECE = 6
REACH = 256
NEG = -1e30
EPS = 1e-5


def rem(value, count):
    return lax.rem(value, count)


def layer_norm(values, gain, bias):
    center = values - jnp.mean(values, axis=1, keepdims=True)
    spread = jnp.mean(center * center, axis=1, keepdims=True)
    return center * lax.rsqrt(spread + EPS) * gain + bias


def gelu(v):
    return v * (0.5 + 0.5 * lax.erf(v * (1.0 / math.sqrt(2.0))))


def kernel(
    hid, wqkv, slen, wo, g1, b1, up, dn, g2, b2, dq, kvc, preq, pused,
    out, dec,
    xb, wob, upb, dnb, kvb, qb, wraw, wcat, ab, ar, atb, nb, rso, rsi, pxo, pxi, cache,
    dqf, dqs, dqb, po, pm, pz, gq, do_, ds_, dor, dsr,
    loc_sem,
    hzs, hzr, hss, hsr,
    wzs, wzr, wss, wsr,
    seeds_s, seeds_r, a1s, a1r, a2s, a2r, b1s, b1r, b2s, b2r,
    halo_s, halo_r,
    aas, aar,
    dqss, dqsr, dcs, dcr, dts, dtr,
    ns, nr, fs, fr,
):
    t = lax.axis_index("tok")
    kv = lax.axis_index("kv")
    z, c = kv // 2, rem(kv, 2)
    y, x = t // NX, rem(t, NX)
    sib = (t, 2 * z + (1 - c))

    def remote(src, dst, ss, rs, dev):
        return pltpu.make_async_remote_copy(
            src_ref=src, dst_ref=dst, send_sem=ss, recv_sem=rs,
            device_id=dev, device_id_type=MESH,
        )

    sent = []

    def start(src, dst, ss, rs, dev):
        copy = remote(src, dst, ss, rs, dev)
        copy.start()
        sent.append(copy)

    def arrived(dst, rs):
        remote(dst, dst, loc_sem.at[0], rs, sib).wait_recv()

    own_rows = pl.ds(pl.multiple_of(kv * 64, 64), 64)
    local = [
        pltpu.make_async_copy(hid, xb.at[own_rows], loc_sem.at[0]),
        pltpu.make_async_copy(wqkv, wraw, loc_sem.at[1]),
        pltpu.make_async_copy(wo, wob.at[own_rows], loc_sem.at[2]),
        pltpu.make_async_copy(up, upb.at[0], loc_sem.at[3]),
        pltpu.make_async_copy(dn, dnb.at[0], loc_sem.at[4]),
        pltpu.make_async_copy(kvc.at[:, 0], cache, loc_sem.at[5]),
    ]
    for copy in local:
        copy.start()

    barrier = pltpu.get_barrier_semaphore()
    peers = [(t, rem(kv + o, NK)) for o in range(1, NK)]
    peers += [(y * NX + rem(x + o, NX), kv) for o in range(1, NX)]
    yup, ydown = (rem(y + 1, NY) * NX + x, kv), (rem(y + NY - 1, NY) * NX + x, kv)
    peers += [yup, ydown]
    tnext, tprev = (rem(t + 1, NT), kv), (rem(t + NT - 1, NT), kv)
    peers += [tnext, tprev]
    for peer in peers:
        pl.semaphore_signal(barrier, inc=1, device_id=peer, device_id_type=MESH)
    pl.semaphore_wait(barrier, len(peers))

    zdev = [(t, 2 * rem(z + 1, NZ) + c), (t, 2 * rem(z + NZ - 1, NZ) + c)]

    def at_hop(d, k):
        return rem(z + NZ - k, NZ) if d == 0 else rem(z + k, NZ)

    def part(zz, core, h):
        return pl.ds(pl.multiple_of((2 * zz + core) * 64 + 32 * h, 32), 32)

    def idx(d, k, h):
        return (d * 4 + k - 1) * 2 + h

    def ring_send(buf, own, zs, zr, k, d, h):
        if k == 4 and h != d:
            return
        zz = at_hop(d, k - 1)
        src = own.at[pl.ds(32 * h, 32)] if k == 1 else buf.at[part(zz, c, h)]
        start(src, buf.at[part(zz, c, h)], zs.at[idx(d, k, h)], zr.at[idx(d, k, h)], zdev[d])

    def ring_first(buf, own, zs, zr, ss, sr):
        for h in range(2):
            for d in range(2):
                ring_send(buf, own, zs, zr, 1, d, h)
        start(own, buf.at[own_rows], ss.at[16], sr.at[16], sib)

    def ring_hop(buf, own, zs, zr, ss, sr, k):
        for h in range(2):
            for d in range(2):
                if k == 4 and h != d:
                    continue
                here = buf.at[part(at_hop(d, k), c, h)]
                arrived(here, zr.at[idx(d, k, h)])
                if k < 4:
                    ring_send(buf, own, zs, zr, k + 1, d, h)
                start(here, here, ss.at[idx(d, k, h)], sr.at[idx(d, k, h)], sib)

    def ring_relayed(buf, sr, k, d):
        for h in range(2):
            if k == 4 and h != d:
                continue
            arrived(buf.at[part(at_hop(d, k), 1 - c, h)], sr.at[idx(d, k, h)])

    hidden = (xb, hid, hzs, hzr, hss, hsr)
    outw = (wob, wo, wzs, wzr, wss, wsr)
    sib_rows = pl.ds(pl.multiple_of((2 * z + 1 - c) * 64, 64), 64)

    ring_first(*hidden)

    up_rows = pl.ds(pl.multiple_of(t * 32, 32), 32)

    def dn_block(xx, yy):
        return (
            pl.ds(pl.multiple_of(64 * xx + 16 * rem(yy, 4), 16), 16),
            pl.ds(pl.multiple_of(512 * (yy // 4), 512), 512),
        )

    dr, dcol = dn_block(x, y)
    for j in range(1, 4):
        dev = (t, rem(kv + NK - 4 * j, NK))
        start(up.at[up_rows, :], upb.at[j, up_rows, :], seeds_s.at[j - 1], seeds_r.at[j - 1], dev)
        start(dn.at[dr, dcol], dnb.at[j, dr, dcol], seeds_s.at[j + 2], seeds_r.at[j + 2], dev)

    qf = dq[...].astype(F32)
    for i in range(8):
        dqf[pl.ds(2 * i, 2), :] = qf[:, 128 * i : 128 * i + 128]
    dqs[...] = dqf[...].astype(BF16)
    dqb[kv] = dqs[...]

    def send_query(o, carry):
        dev = rem(kv + o, NK)
        remote(dqs, dqb.at[kv], dqss.at[o - 1], dqsr.at[kv], (t, dev)).start()
        return carry

    lax.fori_loop(1, NK, send_query, 0)

    first = t * D
    lane = lax.broadcasted_iota(jnp.int32, (1, 128), 1)
    ends = jnp.zeros((1, 128), jnp.int32)

    def add_len(i, ends):
        return ends + jnp.where(lane >= i, slen[i], 0)

    ends = (lax.fori_loop(0, NSEG, add_len, ends) - first).astype(F32)
    floor = (-first).astype(F32)

    local[1].wait()
    zero = jnp.zeros((D, 64), BF16)
    wcat[:, 0:128] = jnp.concatenate([wraw[:, 0, :], zero], axis=1)
    wcat[:, 128:256] = jnp.concatenate([wraw[:, 1, :], wraw[:, 2, :]], axis=1)

    def project(zz):
        rows = pl.ds(pl.multiple_of(zz * 128, 128), 128)
        res = jnp.dot(xb[rows, :], wcat[...], preferred_element_type=F32).astype(BF16)
        qb[rows, :] = res[:, 0:128] * 0.125
        kvb[pl.ds(pl.multiple_of(zz * 128 + REACH, 128), 128), :] = res[:, 128:256]

    ring_hop(*hidden, 1)
    local[0].wait()
    arrived(xb.at[sib_rows], hsr.at[16])
    project(z)

    def xdev(o):
        return (y * NX + rem(x + o, NX), kv)

    ydev = [yup, ydown]

    def y_at(d, k):
        return rem(y + NY - k, NY) if d == 0 else rem(y + k, NY)

    def a2_block(yy, half=None):
        if half is None:
            return upb.at[pl.ds(1, 3), pl.ds(pl.multiple_of(yy * 128, 128), 128), :]
        return upb.at[pl.ds(1, 3), pl.ds(pl.multiple_of(yy * 128 + 64 * half, 64), 64), :]

    def b1_block(yy, half=None):
        r, cc = dn_block(x, yy)
        if half is not None:
            cc = pl.ds(pl.multiple_of(512 * (yy // 4) + 256 * half, 256), 256)
        return dnb.at[pl.ds(1, 3), r, cc]

    def y_send(block, ss, sr, k):
        for d in range(2):
            ref = block(y_at(d, k - 1), d if k == 4 else None)
            start(ref, ref, ss.at[d * 4 + k - 1], sr.at[d * 4 + k - 1], ydev[d])

    def y_wait(block, sr, k):
        for d in range(2):
            arrived(block(y_at(d, k), d if k == 4 else None), sr.at[d * 4 + k - 1])

    for j in range(1, 4):
        arrived(upb.at[j, up_rows, :], seeds_r.at[j - 1])
        arrived(dnb.at[j, dr, dcol], seeds_r.at[j + 2])
    seed = upb.at[pl.ds(1, 3), up_rows, :]
    for o in range(1, NX):
        start(seed, seed, a1s.at[o - 1], a1r.at[o - 1], xdev(o))
    y_send(b1_block, b1s, b1r, 1)

    ring_hop(*hidden, 2)
    for d in range(2):
        ring_relayed(xb, hsr, 1, d)
        project(at_hop(d, 1))

    for o in range(1, NX):
        rows = pl.ds(pl.multiple_of((y * NX + rem(x + NX - o, NX)) * 32, 32), 32)
        arrived(upb.at[pl.ds(1, 3), rows, :], a1r.at[o - 1])
    y_send(a2_block, a2s, a2r, 1)
    y_wait(b1_block, b1r, 1)
    y_send(b1_block, b1s, b1r, 2)

    ring_hop(*hidden, 3)
    for d in range(2):
        ring_relayed(xb, hsr, 2, d)
        project(at_hop(d, 2))
    y_wait(b1_block, b1r, 2)
    y_send(b1_block, b1s, b1r, 3)

    def got_query(o, carry):
        src = rem(kv + o, NK)
        arrived(dqb.at[src], dqsr.at[src])
        return carry

    lax.fori_loop(1, NK, got_query, 0)
    row48 = lax.broadcasted_iota(jnp.int32, (48, 1), 0)
    target = 2 * rem(row48, 8)
    for p in range(NPIECE):
        n = preq[0, p]
        target = target + jnp.where(row48 // 8 == p, 16 * (n // 2) + rem(n, 2), 0)
    col256 = lax.broadcasted_iota(jnp.int32, (48, 256), 1)
    select = (col256 == target).astype(F32).astype(BF16)
    gq[...] = jnp.dot(select, dqb[...].reshape(256, 128), preferred_element_type=F32)
    local[5].wait()
    head16 = lax.broadcasted_iota(jnp.int32, (16, 128), 0)
    lane16 = lax.broadcasted_iota(jnp.int32, (16, 128), 1)
    masks = [head16 == 2 * i + lane16 // 64 for i in range(8)]

    def piece(p, carry):
        g = gq[pl.ds(pl.multiple_of(8 * p, 8), 8), :]
        qbd = jnp.concatenate(
            [jnp.where(masks[i], g[i : i + 1, :], 0.0) for i in range(8)], axis=1
        ).astype(BF16)
        u = lax.dot_general(
            qbd, cache[0, p], (((1,), (1,)), ((), ())), preferred_element_type=F32
        ) * 0.125
        live = lane16 < pused[0, p]
        u = jnp.where(live, u, NEG)
        m = jnp.max(u, axis=1, keepdims=True)
        e = jnp.where(live, jnp.exp(u - m), 0.0)
        s = jnp.sum(e, axis=1, keepdims=True)
        o = jnp.dot(e.astype(BF16), cache[1, p], preferred_element_type=F32)
        for i in range(8):
            po[p, i : i + 1, :] = jnp.sum(
                jnp.where(masks[i], o[:, 128 * i : 128 * i + 128], 0.0), axis=0, keepdims=True
            )
            pm[p, i : i + 1, :] = jnp.sum(jnp.where(masks[i], m, 0.0), axis=0, keepdims=True)
            pz[p, i : i + 1, :] = jnp.sum(jnp.where(masks[i], s, 0.0), axis=0, keepdims=True)
        return carry

    lax.fori_loop(0, NPIECE, piece, 0)
    lane8 = rem(lax.broadcasted_iota(jnp.int32, (8, 128), 1), 64)

    def combine(d, carry):
        values, stats = [], jnp.zeros((8, 128), F32)
        for r in range(2):
            mine = [(preq[0, p] == 2 * d + r) & (pused[0, p] > 0) for p in range(NPIECE)]
            top = jnp.full((8, 128), NEG, F32)
            for p in range(NPIECE):
                top = jnp.maximum(top, jnp.where(mine[p], pm[p], NEG))
            total = jnp.zeros((8, 128), F32)
            value = jnp.zeros((8, 128), F32)
            for p in range(NPIECE):
                factor = jnp.where(mine[p], jnp.exp(pm[p] - top), 0.0)
                total = total + factor * pz[p]
                value = value + factor * po[p]
            values.append(value)
            stats = jnp.where(lane8 == 2 * r, top, jnp.where(lane8 == 2 * r + 1, total, stats))
        do_[d] = jnp.concatenate(values, axis=0).astype(BF16)
        ds_[d] = stats
        return carry

    lax.fori_loop(0, NK, combine, 0)
    dor[kv] = do_[kv]
    dsr[kv] = ds_[kv]

    ring_hop(*hidden, 4)
    for d in range(2):
        ring_relayed(xb, hsr, 3, d)
        project(at_hop(d, 3))
    for d in range(2):
        ring_relayed(xb, hsr, 4, d)
    project(at_hop(0, 4))

    low, high = pl.ds(REACH, REACH), pl.ds(D, REACH)
    start(kvb.at[low], kvb.at[pl.ds(D + REACH, REACH)], halo_s.at[0], halo_r.at[0], tprev)
    start(kvb.at[high], kvb.at[pl.ds(0, REACH)], halo_s.at[1], halo_r.at[1], tnext)

    local[2].wait()
    ring_first(*outw)

    y_wait(a2_block, a2r, 1)
    y_send(a2_block, a2s, a2r, 2)
    y_wait(b1_block, b1r, 3)
    y_send(b1_block, b1s, b1r, 4)

    def attend(b):
        r0 = 256 * b
        q = qb[pl.ds(r0, 256), :]
        keys = kvb[pl.ds(r0, 768), :]
        s = lax.dot_general(q, keys, (((1,), (1,)), ((), ())), preferred_element_type=F32)
        row = (r0 + lax.broadcasted_iota(jnp.int32, (256, 1), 0)).astype(F32)
        begin = jnp.max(jnp.where(ends <= row, ends, floor), axis=1, keepdims=True)
        end = jnp.min(jnp.where(ends > row, ends, 1e9), axis=1, keepdims=True)
        lo = jnp.maximum(begin, row - REACH)
        hi = jnp.minimum(end - 1.0, row + REACH)
        kid = (r0 - REACH + lax.broadcasted_iota(jnp.int32, (1, 768), 1)).astype(F32)
        s = jnp.where((kid >= lo) & (kid <= hi), s, NEG)
        m = jnp.max(s, axis=1, keepdims=True)
        w = jnp.exp(s - m)
        total = jnp.sum(w, axis=1, keepdims=True)
        o = jnp.dot(w.astype(BF16), keys, preferred_element_type=F32) / total
        o = o.reshape(4, 2, 32, 128)
        turned = pltpu.roll(o[:, 0].reshape(128, 128), 64, 1)
        lanes = lax.broadcasted_iota(jnp.int32, (128, 128), 1)
        packed = jnp.where(lanes < 64, turned, o[:, 1].reshape(128, 128)).astype(BF16)
        ab[pl.ds(4 * b, 4)] = packed.reshape(4, 32, 128)

        def send_heads(i, carry):
            d = 4 * b + i

            @pl.when(d != kv)
            def _():
                remote(ab.at[d], ar.at[kv], aas.at[d], aar.at[kv], (t, d)).start()

            @pl.when(d == kv)
            def _():
                ar[kv] = ab[d]

            return carry

        lax.fori_loop(0, 4, send_heads, 0)

    attend(1)
    attend(2)
    ring_hop(*outw, 1)
    arrived(kvb.at[pl.ds(D + REACH, REACH)], halo_r.at[0])
    arrived(kvb.at[pl.ds(0, REACH)], halo_r.at[1])
    attend(0)
    attend(3)
    ring_hop(*outw, 2)

    def send_partial(o, carry):
        dev = rem(kv + o, NK)
        remote(do_.at[dev], dor.at[kv], dcs.at[dev], dcr.at[kv], (t, dev)).start()
        remote(ds_.at[dev], dsr.at[kv], dts.at[dev], dtr.at[kv], (t, dev)).start()
        return carry

    lax.fori_loop(1, NK, send_partial, 0)

    y_wait(a2_block, a2r, 2)
    y_send(a2_block, a2s, a2r, 3)
    y_wait(b1_block, b1r, 4)
    slab = dnb.at[pl.ds(1, 3), pl.ds(pl.multiple_of(64 * x, 64), 64), :]
    for o in range(1, NX):
        start(slab, slab, b2s.at[o - 1], b2r.at[o - 1], xdev(o))

    ring_hop(*outw, 3)
    ring_hop(*outw, 4)
    y_wait(a2_block, a2r, 3)
    y_send(a2_block, a2s, a2r, 4)

    def got_heads(o, carry):
        src = rem(kv + o, NK)
        arrived(ar.at[src], aar.at[src])
        return carry

    lax.fori_loop(1, NK, got_heads, 0)
    lanes32 = lax.broadcasted_iota(jnp.int32, (32, 128), 1)
    for j in range(8):
        m0, m1 = ar[2 * j].astype(F32), ar[2 * j + 1].astype(F32)
        cols = pl.ds(128 * j, 128)
        atb[pl.ds(0, 32), cols] = jnp.where(lanes32 < 64, m0, pltpu.roll(m1, 64, 1)).astype(BF16)
        atb[pl.ds(32, 32), cols] = jnp.where(lanes32 < 64, pltpu.roll(m0, 64, 1), m1).astype(BF16)

    arrived(wob.at[sib_rows], wsr.at[16])
    for k in range(1, 5):
        for d in range(2):
            ring_relayed(wob, wsr, k, d)
    projected = jnp.dot(atb[...], wob[...], preferred_element_type=F32)
    own = xb[own_rows, :].astype(F32)
    normed = layer_norm(own + projected, g1[...], b1[...]).astype(BF16)

    gi = rem(kv, 4)
    odd = rem(z, 2)
    pair = (t, 2 * (z + 1 - 2 * odd) + c)
    nb[pl.ds(pl.multiple_of(gi * 64, 64), 64), :] = normed

    def nrows(zz, core, h):
        return pl.ds(pl.multiple_of((2 * zz + core) * 64 + 32 * h, 32), 32)

    mine = nb.at[pl.ds(pl.multiple_of(gi * 64, 64), 64)]
    for h in range(2):
        ref = nb.at[nrows(odd, c, h)]
        start(ref, ref, ns.at[h], nr.at[h], pair)
    start(mine, mine, ns.at[2], nr.at[2], sib)

    local[3].wait()
    local[4].wait()
    y_wait(a2_block, a2r, 4)
    for o in range(1, NX):
        rows = pl.ds(pl.multiple_of(64 * rem(x + NX - o, NX), 64), 64)
        arrived(dnb.at[pl.ds(1, 3), rows, :], b2r.at[o - 1])

    def ffn(zz):
        rows = nb[pl.ds(pl.multiple_of(zz * 128, 128), 128), :]
        acc = jnp.zeros((128, D), F32)
        for j in range(4):
            units = gelu(jnp.dot(rows, upb[j], preferred_element_type=F32)).astype(BF16)
            acc = acc + jnp.dot(units, dnb[j], preferred_element_type=F32)
        return acc

    arrived(nb.at[pl.ds(pl.multiple_of((2 * odd + 1 - c) * 64, 64), 64)], nr.at[2])
    for h in range(2):
        ref = nb.at[nrows(1 - odd, c, h)]
        arrived(ref, nr.at[h])
        start(ref, ref, ns.at[3 + h], nr.at[3 + h], sib)
    acc = ffn(odd)

    def split(acc):
        low, high = acc[0:64], acc[64:128]
        first = c == 0
        return jnp.where(first, low, high), jnp.where(first, high, low)

    kept, other = split(acc)
    rso[0] = other.astype(BF16)
    start(rso.at[0], rsi.at[0], fs.at[0], fr.at[0], sib)
    for h in range(2):
        arrived(nb.at[nrows(1 - odd, 1 - c, h)], nr.at[3 + h])
    ahead, other = split(ffn(1 - odd))
    rso[1] = other.astype(BF16)
    start(rso.at[1], rsi.at[1], fs.at[1], fr.at[1], sib)
    arrived(rsi.at[1], fr.at[1])
    pxo[...] = (ahead + rsi[1].astype(F32)).astype(BF16)
    start(pxo, pxi, fs.at[2], fr.at[2], pair)

    def got_partial(o, carry):
        src = rem(kv + o, NK)
        arrived(dor.at[src], dcr.at[src])
        arrived(dsr.at[src], dtr.at[src])
        return carry

    lax.fori_loop(1, NK, got_partial, 0)
    stats = dsr[...]
    lane3 = lax.broadcasted_iota(jnp.int32, (NK, 8, 128), 2)

    def spread(at):
        a = jnp.sum(jnp.where(lane3 == at, stats, 0.0), axis=2, keepdims=True)
        b = jnp.sum(jnp.where(lane3 == at + 64, stats, 0.0), axis=2, keepdims=True)
        return jnp.where(lane3 < 64, a, b)

    done = []
    for r in range(2):
        top, total = spread(2 * r), spread(2 * r + 1)
        value = dor[:, 8 * r : 8 * r + 8, :].astype(F32)
        factor = jnp.exp(top - jnp.max(top, axis=0, keepdims=True))
        value = jnp.sum(factor * value, axis=0) / jnp.sum(factor * total, axis=0)
        done.append(jnp.concatenate([value[i : i + 1, :] for i in range(8)], axis=1))
    dec[...] = jnp.concatenate(done, axis=0).astype(BF16)

    arrived(rsi.at[0], fr.at[0])
    kept = kept + rsi[0].astype(F32) + nb[pl.ds(pl.multiple_of(gi * 64, 64), 64), :].astype(F32)
    arrived(pxi, fr.at[2])
    out[...] = layer_norm(kept + pxi[...].astype(F32), g2[...], b2[...]).astype(BF16)

    for copy in sent:
        copy.wait_send()

    def sent_small(o, carry):
        dev = rem(kv + o, NK)
        remote(dqs, dqb.at[kv], dqss.at[o - 1], dqsr.at[kv], (t, dev)).wait_send()
        remote(ab.at[dev], ar.at[kv], aas.at[dev], aar.at[kv], (t, dev)).wait_send()
        remote(do_.at[dev], dor.at[kv], dcs.at[dev], dcr.at[kv], (t, dev)).wait_send()
        remote(ds_.at[dev], dsr.at[kv], dts.at[dev], dtr.at[kv], (t, dev)).wait_send()
        return carry

    lax.fori_loop(1, NK, sent_small, 0)


def body(hid, wqkv, slen, wo, g1, b1, up, dn, g2, b2, dq, kvc, preq, pused):
    vm = pl.BlockSpec(memory_space=pltpu.VMEM)
    hbm = pl.BlockSpec(memory_space=pl.ANY)
    sm = pl.BlockSpec(memory_space=pltpu.SMEM)
    dma = pltpu.SemaphoreType.DMA
    V = pltpu.VMEM
    return pl.pallas_call(
        kernel,
        out_shape=(
            jax.ShapeDtypeStruct((64, D), BF16),
            jax.ShapeDtypeStruct((2, D), BF16),
        ),
        in_specs=[hbm, hbm, sm, hbm, vm, vm, hbm, hbm, vm, vm, vm, hbm, sm, sm],
        out_specs=(vm, vm),
        scratch_shapes=[
            V((D, D), BF16), V((D, D), BF16), V((4, D, 256), BF16), V((4, 256, D), BF16),
            V((D + 2 * REACH, 128), BF16), V((D, 128), BF16), V((D, 3, 64), BF16), V((D, 256), BF16),
            V((NK, 32, 128), BF16), V((NK, 32, 128), BF16), V((64, D), BF16), V((256, D), BF16),
            V((2, 64, D), BF16), V((2, 64, D), BF16), V((64, D), BF16), V((64, D), BF16),
            V((2, NPIECE, 128, D), BF16),
            V((16, 128), F32), V((16, 128), BF16), V((NK, 16, 128), BF16),
            V((NPIECE, 8, 128), F32), V((NPIECE, 8, 128), F32), V((NPIECE, 8, 128), F32), V((48, 128), F32),
            V((NK, 16, 128), BF16), V((NK, 8, 128), F32), V((NK, 16, 128), BF16), V((NK, 8, 128), F32),
            dma((6,)),
            dma((16,)), dma((16,)), dma((17,)), dma((17,)),
            dma((16,)), dma((16,)), dma((17,)), dma((17,)),
            dma((6,)), dma((6,)), dma((3,)), dma((3,)), dma((8,)), dma((8,)),
            dma((8,)), dma((8,)), dma((3,)), dma((3,)),
            dma((2,)), dma((2,)),
            dma((NK,)), dma((NK,)),
            dma((NK,)), dma((NK,)), dma((NK,)), dma((NK,)), dma((NK,)), dma((NK,)),
            dma((5,)), dma((5,)), dma((3,)), dma((3,)),
        ],
        compiler_params=pltpu.CompilerParams(
            collective_id=0, has_side_effects=True, vmem_limit_bytes=48 * 1024 * 1024
        ),
    )(hid, wqkv, slen, wo, g1.reshape(1, D), b1.reshape(1, D), up, dn, g2.reshape(1, D), b2.reshape(1, D), dq, kvc, preq, pused)


def solution(mesh):
    rows = P(("tok", "kv"), None)
    placed = (
        rows, P(None, None, "kv"), P(), P("kv", None), P(), P(), P(None, "kv"), P("kv", None),
        P(), P(), rows, P(None, "tok", "kv", None, None), P("tok", "kv"), P("tok", "kv"),
    )
    return jax.shard_map(
        body, mesh=mesh, in_specs=placed, out_specs=(rows, rows), check_vma=False
    )
```

time: 272 us -> 98.1 us (0.36)
  waiting for transfers between devices: 109 us -> 0 us
  Pallas kernels: 0 us -> 83 us
  blocking collectives: 71.5 us -> 0 us
  matrix products: 21.3 us -> 0 us
  local copies, waits for them, and re-layouts: 34.2 us -> 14 us
  between operations: 14.1 us -> 0.67 us
  other arithmetic: 13.3 us -> 0 us
  starting transfers between devices: 4.3 us -> 0 us
    pallas_call x0 -> x1, Pallas kernels: none -> 83 us  [body(): pl.pallas_call(kernel, out_shape=(jax.ShapeDtypeStruct((64, D), BF16), ja...]
    all_gather x4 -> x0, waiting for transfers between devices: 71 us -> none  [the longest x1 38.6 us: body(): lax.all_gather(normed, 'kv', axis=0, tiled=True)]
    all_gather x3 -> x0, blocking collectives: 56.5 us -> none  [the longest x2 31.8 us: merged(): pieces = jax.tree.map(lambda part: lax.all_gather(part, axis), value)]
    reduce_scatter x1 -> x0, waiting for transfers between devices: 33.8 us -> none  [body(): lax.psum_scatter(jnp.dot(units, down_weight, preferred_element_type=jnp.f...]
    dot_general x11 -> x0, matrix products: 21.3 us -> none  [the longest x1 7.19 us: body(): jnp.dot(units, down_weight, preferred_element_type=jnp.float32)]
    dynamic_slice x19 -> x0, local copies, waits for them, and re-layouts: 16 us -> none  [the longest x15 14.6 us: merged(): lax.scan(lambda subtotal, section: (join(subtotal, section), None), head,...]
    all_to_all x1 -> x0, blocking collectives: 15 us -> none  [body(): lax.all_to_all(attention, 'kv', split_axis=0, concat_axis=1, tiled=True)]
    slice x12 -> x0, local copies, waits for them, and re-layouts: 9.74 us -> none  [the longest x5 5.25 us: merged(): tail = jax.tree.map(lambda part: part[1:], pieces)]
  transfers between devices with their start and end apart: 7 -> 0, of which waited for: 6 -> 0; matrix products, arithmetic and copies ran while one was open for 21% -> 0% of each run, Pallas kernels for 0% -> 0%
where the time goes in v1:
time: 98.1 us; the launch traced here: 97.7 us
  Pallas kernels  83 us (85%)
  local copies, waits for them, and re-layouts  14 us (14%)
    pallas_call x1, Pallas kernels, body(): pl.pallas_call(kernel, out_shape=(jax.ShapeDtypeStruct((64, D), BF16), ja...  83 us
    unnamed x29, local copies, waits for them, and re-layouts  14 us

profile of v1, /device:TPU:1, one launch (start us, length us, event | category | flops | bytes accessed | tf_op | source)
XLA Modules:
  0.0 97.7 jit_solution(2458311385513170911)
XLA Ops:
  0.6 1.6 %copy.16.wqkv = bf16[1024,3,64]{2,1,0:T(4,128)(2,1)S(1)} copy(bf16[1024,3,64]{0,2,1:T(8,128)(2,1)} %param.15) | data formatting | bytes 786432 | tf_op args[1]
  2.2 0.0 copy-start
  2.2 1.9 %copy-done = bf16[2,1,6,128,1024]{4,3,2,1,0:T(8,128)(2,1)S(1)} copy-done((bf16[2,1,6,128,1024]{4,3,2,1,0:T(8,128)(2,1)S(1)}, bf16[2,1,6,128,1024]{4,3,2,1,0:T(8,128)(2,1)}, u32[]{:S(2)}) %copy-start) | copy-done | bytes 3145752
  4.1 0.0 copy-start.1
  4.1 1.0 %copy-done.1 = bf16[1024,256]{1,0:T(8,128)(2,1)S(1)} copy-done((bf16[1024,256]{1,0:T(8,128)(2,1)S(1)}, bf16[1024,256]{1,0:T(8,128)(2,1)}, u32[]{:S(2)}) %copy-start.1) | copy-done | bytes 524312
  5.2 0.0 copy-start.2
  5.2 1.0 %copy-done.2 = bf16[256,1024]{1,0:T(8,128)(2,1)S(1)} copy-done((bf16[256,1024]{1,0:T(8,128)(2,1)S(1)}, bf16[256,1024]{1,0:T(8,128)(2,1)}, u32[]{:S(2)}) %copy-start.2) | copy-done | bytes 524312
  6.2 0.0 copy-start.3
  6.2 0.9 copy-done.3
  7.1 0.0 copy-start.4
  7.1 0.9 copy-done.4
  8.0 0.0 copy-start.5
  8.0 0.7 copy-done.5
  8.7 0.0 copy-start.6
  8.7 0.7 copy-done.6
  9.4 0.0 copy-start.7
  9.4 0.7 copy-done.7
  10.1 0.0 copy-start.8
  10.1 0.7 copy-done.8
  10.8 0.0 copy-start.9
  10.8 0.7 copy-done.9
  11.4 0.0 copy-start.10
  11.4 0.7 copy-done.10
  12.1 0.0 copy-start.11
  12.1 0.7 copy-done.11
  12.8 0.0 copy-start.12
  12.8 0.7 copy-done.12
  13.4 83.0 %shard_map.149 = (bf16[64,1024]{1,0:T(8,128)(2,1)S(1)}, bf16[2,1024]{1,0:T(2,128)(2,1)S(1)}) custom-call(bf16[64,1024]{1,0:T(8,128)(2,1)S(1)} %copy-done.3, bf16[1024,3,64]{2,1,0:T(4,128)(2,1)S(1)} %copy.16.wqkv, s32[48]{0:T(128)S(1)} %copy-done.10, bf16[64,1024]{1,0:T(8,128)(2,1)S(1)} %copy-done.4, f32[1,1024]{1,0:T(1,128)S(1)} %bitcast.4, ...), custom_call_target="tpu_custom_call" | custom-call | tf_op jit(solution)/shard_map/pallas_call | solution.py:531
  96.4 0.7 copy.19
  97.1 0.6 copy.20
Async XLA Ops:
  2.2 1.9 %copy-start = (bf16[2,1,6,128,1024]{4,3,2,1,0:T(8,128)(2,1)S(1)}, bf16[2,1,6,128,1024]{4,3,2,1,0:T(8,128)(2,1)}, u32[]{:S(2)}) copy-start(bf16[2,1,6,128,1024]{4,3,2,1,0:T(8,128)(2,1)} %kvc.1) | copy-start | bytes 9437188
  4.1 1.0 %copy-start.1 = (bf16[1024,256]{1,0:T(8,128)(2,1)S(1)}, bf16[1024,256]{1,0:T(8,128)(2,1)}, u32[]{:S(2)}) copy-start(bf16[1024,256]{1,0:T(8,128)(2,1)} %up.1) | copy-start | bytes 1572868
  5.2 1.0 %copy-start.2 = (bf16[256,1024]{1,0:T(8,128)(2,1)S(1)}, bf16[256,1024]{1,0:T(8,128)(2,1)}, u32[]{:S(2)}) copy-start(bf16[256,1024]{1,0:T(8,128)(2,1)} %dn.1) | copy-start | bytes 1572868
  6.2 0.9 copy-start.3
  7.1 0.9 copy-start.4
  8.0 0.7 copy-start.5
  8.7 0.7 copy-start.6
  9.4 0.7 copy-start.7
  10.1 0.7 copy-start.8
  10.8 0.7 copy-start.9
  11.4 0.7 copy-start.10
  12.1 0.7 copy-start.11
  12.8 0.7 copy-start.12

commit v2 on v1

--- a/solution.py
+++ b/solution.py
@@ -39,14 +39,14 @@
 
 
 def kernel(
-    hid, wqkv, slen, wo, g1, b1, up, dn, g2, b2, dq, kvc, preq, pused,
+    hid, wqkv, slen_in, wo, g1_in, b1_in, up, dn, g2_in, b2_in, dq_in, kvc, preq_in, pused_in,
     out, dec,
-    xb, wob, upb, dnb, kvb, qb, wraw, wcat, ab, ar, atb, nb, rso, rsi, pxo, pxi, cache,
+    g1, b1, g2, b2, dq, slen, preq, pused,
+    xb, wob, upb, dnb, kvb, qb, wcat, wtr, ab, ar, atb, nb, rso, rsi, pxo, pxi, qso, qsi, qxo, qxi, cache,
     dqf, dqs, dqb, po, pm, pz, gq, do_, ds_, dor, dsr,
     loc_sem,
     hzs, hzr, hss, hsr,
-    wzs, wzr, wss, wsr,
-    seeds_s, seeds_r, a1s, a1r, a2s, a2r, b1s, b1r, b2s, b2r,
+    seeds_s, seeds_r, a1s, a1r, a2s, a2r, b1s, b1r, b2s, b2r, w1s, w1r, w2s, w2r, ps, pr,
     halo_s, halo_r,
     aas, aar,
     dqss, dqsr, dcs, dcr, dts, dtr,
@@ -77,14 +77,22 @@
     own_rows = pl.ds(pl.multiple_of(kv * 64, 64), 64)
     local = [
         pltpu.make_async_copy(hid, xb.at[own_rows], loc_sem.at[0]),
-        pltpu.make_async_copy(wqkv, wraw, loc_sem.at[1]),
-        pltpu.make_async_copy(wo, wob.at[own_rows], loc_sem.at[2]),
+        pltpu.make_async_copy(wqkv.at[0], wcat.at[pl.ds(0, 64)], loc_sem.at[1]),
+        pltpu.make_async_copy(wo, wob.at[0], loc_sem.at[2]),
         pltpu.make_async_copy(up, upb.at[0], loc_sem.at[3]),
         pltpu.make_async_copy(dn, dnb.at[0], loc_sem.at[4]),
         pltpu.make_async_copy(kvc.at[:, 0], cache, loc_sem.at[5]),
+        pltpu.make_async_copy(wqkv.at[1], wcat.at[pl.ds(128, 64)], loc_sem.at[6]),
+        pltpu.make_async_copy(wqkv.at[2], wcat.at[pl.ds(192, 64)], loc_sem.at[7]),
+        pltpu.make_async_copy(dq_in, dq, loc_sem.at[8]),
+        pltpu.make_async_copy(slen_in, slen, loc_sem.at[9]),
+        pltpu.make_async_copy(preq_in, preq, loc_sem.at[10]),
+        pltpu.make_async_copy(pused_in, pused, loc_sem.at[11]),
+        pltpu.make_async_copy(g1_in, g1, loc_sem.at[12]),
+        pltpu.make_async_copy(b1_in, b1, loc_sem.at[13]),
+        pltpu.make_async_copy(g2_in, g2, loc_sem.at[14]),
+        pltpu.make_async_copy(b2_in, b2, loc_sem.at[15]),
     ]
-    for copy in local:
-        copy.start()
 
     barrier = pltpu.get_barrier_semaphore()
     peers = [(t, rem(kv + o, NK)) for o in range(1, NK)]
@@ -95,6 +103,8 @@
     peers += [tnext, tprev]
     for peer in peers:
         pl.semaphore_signal(barrier, inc=1, device_id=peer, device_id_type=MESH)
+    for i in (0, 8, 9):
+        local[i].start()
     pl.semaphore_wait(barrier, len(peers))
 
     zdev = [(t, 2 * rem(z + 1, NZ) + c), (t, 2 * rem(z + NZ - 1, NZ) + c)]
@@ -139,25 +149,37 @@
             arrived(buf.at[part(at_hop(d, k), 1 - c, h)], sr.at[idx(d, k, h)])
 
     hidden = (xb, hid, hzs, hzr, hss, hsr)
-    outw = (wob, wo, wzs, wzr, wss, wsr)
     sib_rows = pl.ds(pl.multiple_of((2 * z + 1 - c) * 64, 64), 64)
 
     ring_first(*hidden)
 
     up_rows = pl.ds(pl.multiple_of(t * 32, 32), 32)
 
-    def dn_block(xx, yy):
+    def dn_block(xx, yy, half=None):
+        if half is None:
+            cols = pl.ds(pl.multiple_of(512 * (yy // 4), 512), 512)
+        else:
+            cols = pl.ds(pl.multiple_of(512 * (yy // 4) + 256 * half, 256), 256)
+        return pl.ds(pl.multiple_of(64 * xx + 16 * rem(yy, 4), 16), 16), cols
+
+    def wo_block(xx, yy):
         return (
-            pl.ds(pl.multiple_of(64 * xx + 16 * rem(yy, 4), 16), 16),
-            pl.ds(pl.multiple_of(512 * (yy // 4), 512), 512),
+            pl.ds(pl.multiple_of(16 * rem(yy, 4), 16), 16),
+            pl.ds(pl.multiple_of(256 * xx + 128 * (yy // 4), 128), 128),
         )
 
+    for i in (1, 6, 7, 10, 11, 5, 2, 3, 4, 12, 13, 14, 15):
+        local[i].start()
+
     dr, dcol = dn_block(x, y)
+    wr, wcol = wo_block(x, y)
     for j in range(1, 4):
         dev = (t, rem(kv + NK - 4 * j, NK))
+        start(wo.at[wr, wcol], wob.at[j, wr, wcol], seeds_s.at[j + 5], seeds_r.at[j + 5], dev)
         start(up.at[up_rows, :], upb.at[j, up_rows, :], seeds_s.at[j - 1], seeds_r.at[j - 1], dev)
         start(dn.at[dr, dcol], dnb.at[j, dr, dcol], seeds_s.at[j + 2], seeds_r.at[j + 2], dev)
 
+    local[8].wait()
     qf = dq[...].astype(F32)
     for i in range(8):
         dqf[pl.ds(2 * i, 2), :] = qf[:, 128 * i : 128 * i + 128]
@@ -171,6 +193,7 @@
 
     lax.fori_loop(1, NK, send_query, 0)
 
+    local[9].wait()
     first = t * D
     lane = lax.broadcasted_iota(jnp.int32, (1, 128), 1)
     ends = jnp.zeros((1, 128), jnp.int32)
@@ -181,76 +204,112 @@
     ends = (lax.fori_loop(0, NSEG, add_len, ends) - first).astype(F32)
     floor = (-first).astype(F32)
 
-    local[1].wait()
-    zero = jnp.zeros((D, 64), BF16)
-    wcat[:, 0:128] = jnp.concatenate([wraw[:, 0, :], zero], axis=1)
-    wcat[:, 128:256] = jnp.concatenate([wraw[:, 1, :], wraw[:, 2, :]], axis=1)
+    wcat[pl.ds(64, 64), :] = jnp.zeros((64, D), BF16)
+    for i in (1, 6, 7):
+        local[i].wait()
+
+    for i in range(4):
+        rows = pl.ds(256 * i, 256)
+        wtr[rows, :] = wcat[:, rows].astype(F32).T.astype(BF16)
 
     def project(zz):
         rows = pl.ds(pl.multiple_of(zz * 128, 128), 128)
-        res = jnp.dot(xb[rows, :], wcat[...], preferred_element_type=F32).astype(BF16)
+        res = jnp.dot(xb[rows, :], wtr[...], preferred_element_type=F32).astype(BF16)
         qb[rows, :] = res[:, 0:128] * 0.125
         kvb[pl.ds(pl.multiple_of(zz * 128 + REACH, 128), 128), :] = res[:, 128:256]
 
+    def project_pair(k):
+        def one(d, carry):
+            project(jnp.where(d == 0, rem(z + NZ - k, NZ), rem(z + k, NZ)))
+            return carry
+
+        lax.fori_loop(0, 2, one, 0)
+
     ring_hop(*hidden, 1)
+
+    slots = pl.ds(1, 3)
+    xdev = [(y * NX + rem(x + 1, NX), kv), (y * NX + rem(x + NX - 1, NX), kv)]
+    ydev = [yup, ydown]
+
+    def y_at(d, k):
+        return rem(y + NY - k, NY) if d == 0 else rem(y + k, NY)
+
+    def x_at(d, k):
+        return rem(x + NX - k, NX) if d == 0 else rem(x + k, NX)
+
+    def a2_block(yy, half):
+        if half is None:
+            return upb.at[slots, pl.ds(pl.multiple_of(yy * 128, 128), 128), :]
+        return upb.at[slots, pl.ds(pl.multiple_of(yy * 128 + 64 * half, 64), 64), :]
+
+    def b1_block(yy, half):
+        r, cc = dn_block(x, yy, half)
+        return dnb.at[slots, r, cc]
+
+    def w1_block(yy, half):
+        r, cc = wo_block(x, yy)
+        return wob.at[slots, r, cc]
+
+    def b2_block(xx, half):
+        if half is None:
+            return dnb.at[slots, pl.ds(pl.multiple_of(64 * xx, 64), 64), :]
+        return dnb.at[slots, pl.ds(pl.multiple_of(64 * xx + 32 * half, 32), 32), :]
+
+    def w2_block(xx, half):
+        cols = pl.ds(pl.multiple_of(256 * xx, 256), 256)
+        if half is None:
+            return wob.at[slots, :, cols]
+        return wob.at[slots, pl.ds(32 * half, 32), cols]
+
+    def hop_send(block, at, devs, ss, sr, k, hops, whole=False):
+        for d in range(2):
+            if whole and k == hops and d == 1:
+                continue
+            ref = block(at(d, k - 1), d if k == hops and not whole else None)
+            start(ref, ref, ss.at[d * hops + k - 1], sr.at[d * hops + k - 1], devs[d])
+
+    def hop_wait(block, at, sr, k, hops, whole=False):
+        for d in range(2):
+            if whole and k == hops and d == 1:
+                continue
+            arrived(block(at(d, k), d if k == hops and not whole else None), sr.at[d * hops + k - 1])
+
+    def a2_send(k):
+        hop_send(a2_block, y_at, ydev, a2s, a2r, k, 4)
+
+    def a2_wait(k):
+        hop_wait(a2_block, y_at, a2r, k, 4)
+
+    def b1_send(k):
+        hop_send(w1_block, y_at, ydev, w1s, w1r, k, 4, True)
+        hop_send(b1_block, y_at, ydev, b1s, b1r, k, 4)
+
+    def b1_wait(k):
+        hop_wait(w1_block, y_at, w1r, k, 4, True)
+        hop_wait(b1_block, y_at, b1r, k, 4)
+
+    for j in range(1, 4):
+        arrived(wob.at[j, wr, wcol], seeds_r.at[j + 5])
+        arrived(upb.at[j, up_rows, :], seeds_r.at[j - 1])
+        arrived(dnb.at[j, dr, dcol], seeds_r.at[j + 2])
+    seed = upb.at[slots, up_rows, :]
+    for o in range(1, NX):
+        start(seed, seed, a1s.at[o - 1], a1r.at[o - 1], (y * NX + rem(x + o, NX), kv))
+    b1_send(1)
     local[0].wait()
     arrived(xb.at[sib_rows], hsr.at[16])
     project(z)
 
-    def xdev(o):
-        return (y * NX + rem(x + o, NX), kv)
-
-    ydev = [yup, ydown]
-
-    def y_at(d, k):
-        return rem(y + NY - k, NY) if d == 0 else rem(y + k, NY)
-
-    def a2_block(yy, half=None):
-        if half is None:
-            return upb.at[pl.ds(1, 3), pl.ds(pl.multiple_of(yy * 128, 128), 128), :]
-        return upb.at[pl.ds(1, 3), pl.ds(pl.multiple_of(yy * 128 + 64 * half, 64), 64), :]
-
-    def b1_block(yy, half=None):
-        r, cc = dn_block(x, yy)
-        if half is not None:
-            cc = pl.ds(pl.multiple_of(512 * (yy // 4) + 256 * half, 256), 256)
-        return dnb.at[pl.ds(1, 3), r, cc]
-
-    def y_send(block, ss, sr, k):
-        for d in range(2):
-            ref = block(y_at(d, k - 1), d if k == 4 else None)
-            start(ref, ref, ss.at[d * 4 + k - 1], sr.at[d * 4 + k - 1], ydev[d])
-
-    def y_wait(block, sr, k):
-        for d in range(2):
-            arrived(block(y_at(d, k), d if k == 4 else None), sr.at[d * 4 + k - 1])
-
-    for j in range(1, 4):
-        arrived(upb.at[j, up_rows, :], seeds_r.at[j - 1])
-        arrived(dnb.at[j, dr, dcol], seeds_r.at[j + 2])
-    seed = upb.at[pl.ds(1, 3), up_rows, :]
+    ring_hop(*hidden, 2)
     for o in range(1, NX):
-        start(seed, seed, a1s.at[o - 1], a1r.at[o - 1], xdev(o))
-    y_send(b1_block, b1s, b1r, 1)
-
-    ring_hop(*hidden, 2)
+        rows = pl.ds(pl.multiple_of((y * NX + rem(x + NX - o, NX)) * 32, 32), 32)
+        arrived(upb.at[slots, rows, :], a1r.at[o - 1])
+    a2_send(1)
+    b1_wait(1)
+    b1_send(2)
     for d in range(2):
         ring_relayed(xb, hsr, 1, d)
-        project(at_hop(d, 1))
-
-    for o in range(1, NX):
-        rows = pl.ds(pl.multiple_of((y * NX + rem(x + NX - o, NX)) * 32, 32), 32)
-        arrived(upb.at[pl.ds(1, 3), rows, :], a1r.at[o - 1])
-    y_send(a2_block, a2s, a2r, 1)
-    y_wait(b1_block, b1r, 1)
-    y_send(b1_block, b1s, b1r, 2)
-
-    ring_hop(*hidden, 3)
-    for d in range(2):
-        ring_relayed(xb, hsr, 2, d)
-        project(at_hop(d, 2))
-    y_wait(b1_block, b1r, 2)
-    y_send(b1_block, b1s, b1r, 3)
+    project_pair(1)
 
     def got_query(o, carry):
         src = rem(kv + o, NK)
@@ -258,6 +317,8 @@
         return carry
 
     lax.fori_loop(1, NK, got_query, 0)
+    local[10].wait()
+    local[11].wait()
     row48 = lax.broadcasted_iota(jnp.int32, (48, 1), 0)
     target = 2 * rem(row48, 8)
     for p in range(NPIECE):
@@ -294,6 +355,13 @@
         return carry
 
     lax.fori_loop(0, NPIECE, piece, 0)
+
+    ring_hop(*hidden, 3)
+    b1_wait(2)
+    b1_send(3)
+    for d in range(2):
+        ring_relayed(xb, hsr, 2, d)
+    project_pair(2)
     lane8 = rem(lax.broadcasted_iota(jnp.int32, (8, 128), 1), 64)
 
     def combine(d, carry):
@@ -320,9 +388,13 @@
     dsr[kv] = ds_[kv]
 
     ring_hop(*hidden, 4)
+    b1_wait(3)
+    b1_send(4)
+    a2_wait(1)
+    a2_send(2)
     for d in range(2):
         ring_relayed(xb, hsr, 3, d)
-        project(at_hop(d, 3))
+    project_pair(3)
     for d in range(2):
         ring_relayed(xb, hsr, 4, d)
     project(at_hop(0, 4))
@@ -331,16 +403,21 @@
     start(kvb.at[low], kvb.at[pl.ds(D + REACH, REACH)], halo_s.at[0], halo_r.at[0], tprev)
     start(kvb.at[high], kvb.at[pl.ds(0, REACH)], halo_s.at[1], halo_r.at[1], tnext)
 
-    local[2].wait()
-    ring_first(*outw)
-
-    y_wait(a2_block, a2r, 1)
-    y_send(a2_block, a2s, a2r, 2)
-    y_wait(b1_block, b1r, 3)
-    y_send(b1_block, b1s, b1r, 4)
+    def send_partial(o, carry):
+        dev = rem(kv + o, NK)
+        remote(do_.at[dev], dor.at[kv], dcs.at[dev], dcr.at[kv], (t, dev)).start()
+        remote(ds_.at[dev], dsr.at[kv], dts.at[dev], dtr.at[kv], (t, dev)).start()
+        return carry
+
+    lax.fori_loop(1, NK, send_partial, 0)
+
+
+    gi = rem(kv, 4)
+    odd = rem(z, 2)
+    q4 = z // 2
 
     def attend(b):
-        r0 = 256 * b
+        r0 = pl.multiple_of(256 * b, 256)
         q = qb[pl.ds(r0, 256), :]
         keys = kvb[pl.ds(r0, 768), :]
         s = lax.dot_general(q, keys, (((1,), (1,)), ((), ())), preferred_element_type=F32)
@@ -355,80 +432,82 @@
         w = jnp.exp(s - m)
         total = jnp.sum(w, axis=1, keepdims=True)
         o = jnp.dot(w.astype(BF16), keys, preferred_element_type=F32) / total
-        o = o.reshape(4, 2, 32, 128)
-        turned = pltpu.roll(o[:, 0].reshape(128, 128), 64, 1)
         lanes = lax.broadcasted_iota(jnp.int32, (128, 128), 1)
-        packed = jnp.where(lanes < 64, turned, o[:, 1].reshape(128, 128)).astype(BF16)
-        ab[pl.ds(4 * b, 4)] = packed.reshape(4, 32, 128)
-
-        def send_heads(i, carry):
-            d = 4 * b + i
-
-            @pl.when(d != kv)
-            def _():
-                remote(ab.at[d], ar.at[kv], aas.at[d], aar.at[kv], (t, d)).start()
-
-            @pl.when(d == kv)
-            def _():
-                ar[kv] = ab[d]
-
-            return carry
-
-        lax.fori_loop(0, 4, send_heads, 0)
-
-    attend(1)
-    attend(2)
-    ring_hop(*outw, 1)
+        turned = pltpu.roll(o[0:128], 64, 1)
+        packed = jnp.where(lanes < 64, turned, o[128:256]).astype(BF16)
+        ab[b] = packed
+        slot = rem(q4 - b + 4, 4)
+
+        @pl.when(b != q4)
+        def _():
+            remote(ab.at[b], ar.at[slot], aas.at[b], aar.at[slot], (t, 4 * b + gi)).start()
+
+        @pl.when(b == q4)
+        def _():
+            ar[0] = packed
+
+    def inner(i, carry):
+        attend(1 + i)
+        return carry
+
+    def outer(i, carry):
+        attend(3 * i)
+        return carry
+
+    b1_wait(4)
+    hop_send(w2_block, x_at, xdev, w2s, w2r, 1, 2)
+    hop_send(b2_block, x_at, xdev, b2s, b2r, 1, 2)
+    lax.fori_loop(0, 2, inner, 0)
+    hop_wait(w2_block, x_at, w2r, 1, 2)
+    hop_send(w2_block, x_at, xdev, w2s, w2r, 2, 2)
+    a2_wait(2)
+    a2_send(3)
     arrived(kvb.at[pl.ds(D + REACH, REACH)], halo_r.at[0])
     arrived(kvb.at[pl.ds(0, REACH)], halo_r.at[1])
-    attend(0)
-    attend(3)
-    ring_hop(*outw, 2)
-
-    def send_partial(o, carry):
-        dev = rem(kv + o, NK)
-        remote(do_.at[dev], dor.at[kv], dcs.at[dev], dcr.at[kv], (t, dev)).start()
-        remote(ds_.at[dev], dsr.at[kv], dts.at[dev], dtr.at[kv], (t, dev)).start()
-        return carry
-
-    lax.fori_loop(1, NK, send_partial, 0)
-
-    y_wait(a2_block, a2r, 2)
-    y_send(a2_block, a2s, a2r, 3)
-    y_wait(b1_block, b1r, 4)
-    slab = dnb.at[pl.ds(1, 3), pl.ds(pl.multiple_of(64 * x, 64), 64), :]
-    for o in range(1, NX):
-        start(slab, slab, b2s.at[o - 1], b2r.at[o - 1], xdev(o))
-
-    ring_hop(*outw, 3)
-    ring_hop(*outw, 4)
-    y_wait(a2_block, a2r, 3)
-    y_send(a2_block, a2s, a2r, 4)
-
-    def got_heads(o, carry):
-        src = rem(kv + o, NK)
-        arrived(ar.at[src], aar.at[src])
-        return carry
-
-    lax.fori_loop(1, NK, got_heads, 0)
-    lanes32 = lax.broadcasted_iota(jnp.int32, (32, 128), 1)
-    for j in range(8):
+    lax.fori_loop(0, 2, outer, 0)
+
+    for j in range(1, 4):
+        arrived(ar.at[j], aar.at[j])
+    local[2].wait()
+    hop_wait(w2_block, x_at, w2r, 2, 2)
+
+    lanes = lax.broadcasted_iota(jnp.int32, (128, 128), 1)
+    for j in range(2):
         m0, m1 = ar[2 * j].astype(F32), ar[2 * j + 1].astype(F32)
         cols = pl.ds(128 * j, 128)
-        atb[pl.ds(0, 32), cols] = jnp.where(lanes32 < 64, m0, pltpu.roll(m1, 64, 1)).astype(BF16)
-        atb[pl.ds(32, 32), cols] = jnp.where(lanes32 < 64, pltpu.roll(m0, 64, 1), m1).astype(BF16)
-
-    arrived(wob.at[sib_rows], wsr.at[16])
-    for k in range(1, 5):
-        for d in range(2):
-            ring_relayed(wob, wsr, k, d)
-    projected = jnp.dot(atb[...], wob[...], preferred_element_type=F32)
-    own = xb[own_rows, :].astype(F32)
-    normed = layer_norm(own + projected, g1[...], b1[...]).astype(BF16)
-
-    gi = rem(kv, 4)
-    odd = rem(z, 2)
+        atb[0, :, cols] = jnp.where(lanes < 64, m0, pltpu.roll(m1, 64, 1)).astype(BF16)
+        atb[1, :, cols] = jnp.where(lanes < 64, pltpu.roll(m0, 64, 1), m1).astype(BF16)
+
     pair = (t, 2 * (z + 1 - 2 * odd) + c)
+
+    def split(acc):
+        low, high = acc[0:64], acc[64:128]
+        first = c == 0
+        return jnp.where(first, low, high), jnp.where(first, high, low)
+
+    def heads(zz):
+        return jnp.dot(atb[zz], wob[...].reshape(256, D), preferred_element_type=F32)
+
+    ahead, other = split(heads(1 - odd))
+    qso[1] = other.astype(BF16)
+    start(qso.at[1], qsi.at[1], ps.at[1], pr.at[1], sib)
+    keep, other = split(heads(odd))
+    qso[0] = other.astype(BF16)
+    start(qso.at[0], qsi.at[0], ps.at[0], pr.at[0], sib)
+    a2_wait(3)
+    a2_send(4)
+    arrived(qsi.at[1], pr.at[1])
+    qxo[...] = (ahead + qsi[1].astype(F32)).astype(BF16)
+    start(qxo, qxi, ps.at[2], pr.at[2], pair)
+    arrived(qsi.at[0], pr.at[0])
+    keep = keep + qsi[0].astype(F32) + xb[own_rows, :].astype(F32)
+    local[12].wait()
+    local[13].wait()
+    hop_wait(b2_block, x_at, b2r, 1, 2)
+    hop_send(b2_block, x_at, xdev, b2s, b2r, 2, 2)
+    arrived(qxi, pr.at[2])
+    normed = layer_norm(keep + qxi[...].astype(F32), g1[...], b1[...]).astype(BF16)
+
     nb[pl.ds(pl.multiple_of(gi * 64, 64), 64), :] = normed
 
     def nrows(zz, core, h):
@@ -440,12 +519,15 @@
         start(ref, ref, ns.at[h], nr.at[h], pair)
     start(mine, mine, ns.at[2], nr.at[2], sib)
 
+    arrived(nb.at[pl.ds(pl.multiple_of((2 * odd + 1 - c) * 64, 64), 64)], nr.at[2])
+    for h in range(2):
+        ref = nb.at[nrows(1 - odd, c, h)]
+        arrived(ref, nr.at[h])
+        start(ref, ref, ns.at[3 + h], nr.at[3 + h], sib)
     local[3].wait()
     local[4].wait()
-    y_wait(a2_block, a2r, 4)
-    for o in range(1, NX):
-        rows = pl.ds(pl.multiple_of(64 * rem(x + NX - o, NX), 64), 64)
-        arrived(dnb.at[pl.ds(1, 3), rows, :], b2r.at[o - 1])
+    a2_wait(4)
+    hop_wait(b2_block, x_at, b2r, 2, 2)
 
     def ffn(zz):
         rows = nb[pl.ds(pl.multiple_of(zz * 128, 128), 128), :]
@@ -455,17 +537,7 @@
             acc = acc + jnp.dot(units, dnb[j], preferred_element_type=F32)
         return acc
 
-    arrived(nb.at[pl.ds(pl.multiple_of((2 * odd + 1 - c) * 64, 64), 64)], nr.at[2])
-    for h in range(2):
-        ref = nb.at[nrows(1 - odd, c, h)]
-        arrived(ref, nr.at[h])
-        start(ref, ref, ns.at[3 + h], nr.at[3 + h], sib)
     acc = ffn(odd)
-
-    def split(acc):
-        low, high = acc[0:64], acc[64:128]
-        first = c == 0
-        return jnp.where(first, low, high), jnp.where(first, high, low)
 
     kept, other = split(acc)
     rso[0] = other.astype(BF16)
@@ -506,6 +578,8 @@
     arrived(rsi.at[0], fr.at[0])
     kept = kept + rsi[0].astype(F32) + nb[pl.ds(pl.multiple_of(gi * 64, 64), 64), :].astype(F32)
     arrived(pxi, fr.at[2])
+    local[14].wait()
+    local[15].wait()
     out[...] = layer_norm(kept + pxi[...].astype(F32), g2[...], b2[...]).astype(BF16)
 
     for copy in sent:
@@ -514,18 +588,25 @@
     def sent_small(o, carry):
         dev = rem(kv + o, NK)
         remote(dqs, dqb.at[kv], dqss.at[o - 1], dqsr.at[kv], (t, dev)).wait_send()
-        remote(ab.at[dev], ar.at[kv], aas.at[dev], aar.at[kv], (t, dev)).wait_send()
         remote(do_.at[dev], dor.at[kv], dcs.at[dev], dcr.at[kv], (t, dev)).wait_send()
         remote(ds_.at[dev], dsr.at[kv], dts.at[dev], dtr.at[kv], (t, dev)).wait_send()
         return carry
 
     lax.fori_loop(1, NK, sent_small, 0)
 
+    def sent_heads(o, carry):
+        b = rem(q4 + o, 4)
+        slot = rem(q4 - b + 4, 4)
+        remote(ab.at[b], ar.at[slot], aas.at[b], aar.at[slot], (t, 4 * b + gi)).wait_send()
+        return carry
+
+    lax.fori_loop(1, 4, sent_heads, 0)
+
 
 def body(hid, wqkv, slen, wo, g1, b1, up, dn, g2, b2, dq, kvc, preq, pused):
     vm = pl.BlockSpec(memory_space=pltpu.VMEM)
-    hbm = pl.BlockSpec(memory_space=pl.ANY)
-    sm = pl.BlockSpec(memory_space=pltpu.SMEM)
+    hbm = pl.BlockSpec(memory_space=pltpu.HBM)
+    S = pltpu.SMEM
     dma = pltpu.SemaphoreType.DMA
     V = pltpu.VMEM
     return pl.pallas_call(
@@ -534,31 +615,33 @@
             jax.ShapeDtypeStruct((64, D), BF16),
             jax.ShapeDtypeStruct((2, D), BF16),
         ),
-        in_specs=[hbm, hbm, sm, hbm, vm, vm, hbm, hbm, vm, vm, vm, hbm, sm, sm],
+        in_specs=[hbm] * 14,
         out_specs=(vm, vm),
         scratch_shapes=[
-            V((D, D), BF16), V((D, D), BF16), V((4, D, 256), BF16), V((4, 256, D), BF16),
-            V((D + 2 * REACH, 128), BF16), V((D, 128), BF16), V((D, 3, 64), BF16), V((D, 256), BF16),
-            V((NK, 32, 128), BF16), V((NK, 32, 128), BF16), V((64, D), BF16), V((256, D), BF16),
+            V((1, D), F32), V((1, D), F32), V((1, D), F32), V((1, D), F32), V((2, D), BF16),
+            S((NSEG,), jnp.int32), S((1, NPIECE), jnp.int32), S((1, NPIECE), jnp.int32),
+            V((D, D), BF16), V((4, 64, D), BF16), V((4, D, 256), BF16), V((4, 256, D), BF16),
+            V((D + 2 * REACH, 128), BF16), V((D, 128), BF16), V((256, D), BF16), V((D, 256), BF16),
+            V((4, 128, 128), BF16), V((4, 128, 128), BF16), V((2, 128, 256), BF16), V((256, D), BF16),
+            V((2, 64, D), BF16), V((2, 64, D), BF16), V((64, D), BF16), V((64, D), BF16),
             V((2, 64, D), BF16), V((2, 64, D), BF16), V((64, D), BF16), V((64, D), BF16),
             V((2, NPIECE, 128, D), BF16),
             V((16, 128), F32), V((16, 128), BF16), V((NK, 16, 128), BF16),
             V((NPIECE, 8, 128), F32), V((NPIECE, 8, 128), F32), V((NPIECE, 8, 128), F32), V((48, 128), F32),
             V((NK, 16, 128), BF16), V((NK, 8, 128), F32), V((NK, 16, 128), BF16), V((NK, 8, 128), F32),
-            dma((6,)),
+            dma((16,)),
             dma((16,)), dma((16,)), dma((17,)), dma((17,)),
-            dma((16,)), dma((16,)), dma((17,)), dma((17,)),
-            dma((6,)), dma((6,)), dma((3,)), dma((3,)), dma((8,)), dma((8,)),
-            dma((8,)), dma((8,)), dma((3,)), dma((3,)),
+            dma((9,)), dma((9,)), dma((3,)), dma((3,)), dma((8,)), dma((8,)),
+            dma((8,)), dma((8,)), dma((4,)), dma((4,)), dma((8,)), dma((8,)), dma((4,)), dma((4,)), dma((3,)), dma((3,)),
             dma((2,)), dma((2,)),
-            dma((NK,)), dma((NK,)),
+            dma((4,)), dma((4,)),
             dma((NK,)), dma((NK,)), dma((NK,)), dma((NK,)), dma((NK,)), dma((NK,)),
             dma((5,)), dma((5,)), dma((3,)), dma((3,)),
         ],
         compiler_params=pltpu.CompilerParams(
-            collective_id=0, has_side_effects=True, vmem_limit_bytes=48 * 1024 * 1024
+            collective_id=0, has_side_effects=True, vmem_limit_bytes=65400 * 1024
         ),
-    )(hid, wqkv, slen, wo, g1.reshape(1, D), b1.reshape(1, D), up, dn, g2.reshape(1, D), b2.reshape(1, D), dq, kvc, preq, pused)
+    )(hid, jnp.transpose(wqkv, (1, 2, 0)), slen, wo, g1.reshape(1, D), b1.reshape(1, D), up, dn, g2.reshape(1, D), b2.reshape(1, D), dq, kvc, preq, pused)
 
 
 def solution(mesh):

time: 98.1 us -> 82.1 us (0.84)
  local copies, waits for them, and re-layouts: 14 us -> 2.85 us
  Pallas kernels: 83 us -> 78.4 us
    unnamed x29 -> x2, local copies, waits for them, and re-layouts: 14 us -> 2.85 us
    pallas_call x1, Pallas kernels: 83 us -> 78.4 us  [body(): pl.pallas_call(kernel, out_shape=(jax.ShapeDtypeStruct((64, D), BF16), ja...]
where the time goes in v2:
time: 82.1 us; the launch traced here: 81.9 us
  Pallas kernels  78.4 us (95%)
  local copies, waits for them, and re-layouts  2.85 us (3%)
    pallas_call x1, Pallas kernels, body(): pl.pallas_call(kernel, out_shape=(jax.ShapeDtypeStruct((64, D), BF16), ja...  78.4 us
    unnamed x2, local copies, waits for them, and re-layouts  2.85 us

profile of v2, /device:TPU:1, one launch (start us, length us, event | category | flops | bytes accessed | tf_op | source)
XLA Modules:
  0.0 81.9 jit_solution(13374174952899916684)
XLA Ops:
  0.6 78.4 %shard_map.149 = (bf16[64,1024]{1,0:T(8,128)(2,1)}, bf16[2,1024]{1,0:T(2,128)(2,1)}) custom-call(bf16[64,1024]{1,0:T(8,128)(2,1)} %hid.1, bf16[3,64,1024]{2,1,0:T(8,128)(2,1)} %bitcast.5, s32[48]{0:T(128)} %slen_in.1, bf16[64,1024]{1,0:T(8,128)(2,1)} %wo.1, f32[1,1024]{1,0:T(1,128)} %bitcast.6, f32[1,1024]{1,0:T(1,128)} %bitcast.7, bf16[1024,256]{1,0:T(8,128)(2,1)} %up.1, ...), custom_call_target="tpu_custom_call" | custom-call | tf_op jit(solution)/shard_map/pallas_call | solution.py:612
  79.0 1.6 %copy.18 = bf16[64,1024]{1,0:T(8,128)(2,1)} copy(bf16[64,1024]{1,0:T(8,128)(2,1)} %get-tuple-element.4) | data formatting | bytes 262144
  80.6 1.3 %copy.19 = bf16[2,1024]{1,0:T(2,128)(2,1)} copy(bf16[2,1024]{1,0:T(2,128)(2,1)} %get-tuple-element.5) | data formatting | bytes 8192

commit v3 on v2

--- a/solution.py
+++ b/solution.py
@@ -98,7 +98,7 @@
     peers = [(t, rem(kv + o, NK)) for o in range(1, NK)]
     peers += [(y * NX + rem(x + o, NX), kv) for o in range(1, NX)]
     yup, ydown = (rem(y + 1, NY) * NX + x, kv), (rem(y + NY - 1, NY) * NX + x, kv)
-    peers += [yup, ydown]
+    peers += [(rem(y + o, NY) * NX + x, kv) for o in range(1, NY)]
     tnext, tprev = (rem(t + 1, NT), kv), (rem(t + NT - 1, NT), kv)
     peers += [tnext, tprev]
     for peer in peers:
@@ -112,46 +112,38 @@
     def at_hop(d, k):
         return rem(z + NZ - k, NZ) if d == 0 else rem(z + k, NZ)
 
-    def part(zz, core, h):
-        return pl.ds(pl.multiple_of((2 * zz + core) * 64 + 32 * h, 32), 32)
-
-    def idx(d, k, h):
-        return (d * 4 + k - 1) * 2 + h
-
-    def ring_send(buf, own, zs, zr, k, d, h):
-        if k == 4 and h != d:
-            return
-        zz = at_hop(d, k - 1)
-        src = own.at[pl.ds(32 * h, 32)] if k == 1 else buf.at[part(zz, c, h)]
-        start(src, buf.at[part(zz, c, h)], zs.at[idx(d, k, h)], zr.at[idx(d, k, h)], zdev[d])
+    def part(zz, core, half=None):
+        first = (2 * zz + core) * 64
+        if half is None:
+            return pl.ds(pl.multiple_of(first, 64), 64)
+        return pl.ds(pl.multiple_of(first + 32 * half, 32), 32)
+
+    def ring_send(buf, own, zs, zr, k, d):
+        zz, i = at_hop(d, k - 1), d * 4 + k - 1
+        rows = part(zz, c, d if k == 4 else None)
+        src = own if k == 1 else buf.at[rows]
+        start(src, buf.at[rows], zs.at[i], zr.at[i], zdev[d])
 
     def ring_first(buf, own, zs, zr, ss, sr):
-        for h in range(2):
-            for d in range(2):
-                ring_send(buf, own, zs, zr, 1, d, h)
-        start(own, buf.at[own_rows], ss.at[16], sr.at[16], sib)
+        for d in range(2):
+            ring_send(buf, own, zs, zr, 1, d)
+        start(own, buf.at[own_rows], ss.at[8], sr.at[8], sib)
 
     def ring_hop(buf, own, zs, zr, ss, sr, k):
-        for h in range(2):
-            for d in range(2):
-                if k == 4 and h != d:
-                    continue
-                here = buf.at[part(at_hop(d, k), c, h)]
-                arrived(here, zr.at[idx(d, k, h)])
-                if k < 4:
-                    ring_send(buf, own, zs, zr, k + 1, d, h)
-                start(here, here, ss.at[idx(d, k, h)], sr.at[idx(d, k, h)], sib)
+        for d in range(2):
+            i = d * 4 + k - 1
+            here = buf.at[part(at_hop(d, k), c, d if k == 4 else None)]
+            arrived(here, zr.at[i])
+            if k < 4:
+                ring_send(buf, own, zs, zr, k + 1, d)
+            start(here, here, ss.at[i], sr.at[i], sib)
 
     def ring_relayed(buf, sr, k, d):
-        for h in range(2):
-            if k == 4 and h != d:
-                continue
-            arrived(buf.at[part(at_hop(d, k), 1 - c, h)], sr.at[idx(d, k, h)])
+        arrived(buf.at[part(at_hop(d, k), 1 - c, d if k == 4 else None)], sr.at[d * 4 + k - 1])
 
     hidden = (xb, hid, hzs, hzr, hss, hsr)
     sib_rows = pl.ds(pl.multiple_of((2 * z + 1 - c) * 64, 64), 64)
 
-    ring_first(*hidden)
 
     up_rows = pl.ds(pl.multiple_of(t * 32, 32), 32)
 
@@ -171,13 +163,16 @@
     for i in (1, 6, 7, 10, 11, 5, 2, 3, 4, 12, 13, 14, 15):
         local[i].start()
 
+    sign = 2 * rem(z, 2) - 1
     dr, dcol = dn_block(x, y)
     wr, wcol = wo_block(x, y)
     for j in range(1, 4):
-        dev = (t, rem(kv + NK - 4 * j, NK))
+        dev = (t, 2 * rem(z + NZ + sign * (j if j != 2 else -2), NZ) + c)
         start(wo.at[wr, wcol], wob.at[j, wr, wcol], seeds_s.at[j + 5], seeds_r.at[j + 5], dev)
         start(up.at[up_rows, :], upb.at[j, up_rows, :], seeds_s.at[j - 1], seeds_r.at[j - 1], dev)
         start(dn.at[dr, dcol], dnb.at[j, dr, dcol], seeds_s.at[j + 2], seeds_r.at[j + 2], dev)
+
+    ring_first(*hidden)
 
     local[8].wait()
     qf = dq[...].astype(F32)
@@ -281,11 +276,9 @@
         hop_wait(a2_block, y_at, a2r, k, 4)
 
     def b1_send(k):
-        hop_send(w1_block, y_at, ydev, w1s, w1r, k, 4, True)
         hop_send(b1_block, y_at, ydev, b1s, b1r, k, 4)
 
     def b1_wait(k):
-        hop_wait(w1_block, y_at, w1r, k, 4, True)
         hop_wait(b1_block, y_at, b1r, k, 4)
 
     for j in range(1, 4):
@@ -295,9 +288,12 @@
     seed = upb.at[slots, up_rows, :]
     for o in range(1, NX):
         start(seed, seed, a1s.at[o - 1], a1r.at[o - 1], (y * NX + rem(x + o, NX), kv))
+    shard = wob.at[slots, wr, wcol]
+    for o in range(1, NY):
+        start(shard, shard, w1s.at[o - 1], w1r.at[o - 1], (rem(y + o, NY) * NX + x, kv))
     b1_send(1)
     local[0].wait()
-    arrived(xb.at[sib_rows], hsr.at[16])
+    arrived(xb.at[sib_rows], hsr.at[8])
     project(z)
 
     ring_hop(*hidden, 2)
@@ -357,6 +353,11 @@
     lax.fori_loop(0, NPIECE, piece, 0)
 
     ring_hop(*hidden, 3)
+    for o in range(1, NY):
+        arrived(w1_block(rem(y + NY - o, NY), None), w1r.at[o - 1])
+    part_cols = w2_block(x, None)
+    for o in range(1, NX):
+        start(part_cols, part_cols, w2s.at[o - 1], w2r.at[o - 1], (y * NX + rem(x + o, NX), kv))
     b1_wait(2)
     b1_send(3)
     for d in range(2):
@@ -415,6 +416,13 @@
     gi = rem(kv, 4)
     odd = rem(z, 2)
     q4 = z // 2
+
+    def holder(b):
+        step = rem(sign * (b - q4) + 4, 4)
+        turn = (step - 1) * (step - 2) // 2
+        slot = 1 + 2 * (step - 1) - 3 * turn
+        ahead = 1 + 2 * (step - 1) - 7 * turn
+        return rem(slot + 4, 4), (t, 2 * rem(z + 2 * NZ + sign * ahead, NZ) + c)
 
     def attend(b):
         r0 = pl.multiple_of(256 * b, 256)
@@ -436,11 +444,11 @@
         turned = pltpu.roll(o[0:128], 64, 1)
         packed = jnp.where(lanes < 64, turned, o[128:256]).astype(BF16)
         ab[b] = packed
-        slot = rem(q4 - b + 4, 4)
+        slot, dev = holder(b)
 
         @pl.when(b != q4)
         def _():
-            remote(ab.at[b], ar.at[slot], aas.at[b], aar.at[slot], (t, 4 * b + gi)).start()
+            remote(ab.at[b], ar.at[slot], aas.at[b], aar.at[slot], dev).start()
 
         @pl.when(b == q4)
         def _():
@@ -455,11 +463,8 @@
         return carry
 
     b1_wait(4)
-    hop_send(w2_block, x_at, xdev, w2s, w2r, 1, 2)
     hop_send(b2_block, x_at, xdev, b2s, b2r, 1, 2)
     lax.fori_loop(0, 2, inner, 0)
-    hop_wait(w2_block, x_at, w2r, 1, 2)
-    hop_send(w2_block, x_at, xdev, w2s, w2r, 2, 2)
     a2_wait(2)
     a2_send(3)
     arrived(kvb.at[pl.ds(D + REACH, REACH)], halo_r.at[0])
@@ -469,7 +474,8 @@
     for j in range(1, 4):
         arrived(ar.at[j], aar.at[j])
     local[2].wait()
-    hop_wait(w2_block, x_at, w2r, 2, 2)
+    for o in range(1, NX):
+        arrived(w2_block(rem(x + NX - o, NX), None), w2r.at[o - 1])
 
     lanes = lax.broadcasted_iota(jnp.int32, (128, 128), 1)
     for j in range(2):
@@ -537,16 +543,14 @@
             acc = acc + jnp.dot(units, dnb[j], preferred_element_type=F32)
         return acc
 
-    acc = ffn(odd)
-
-    kept, other = split(acc)
-    rso[0] = other.astype(BF16)
-    start(rso.at[0], rsi.at[0], fs.at[0], fr.at[0], sib)
     for h in range(2):
         arrived(nb.at[nrows(1 - odd, 1 - c, h)], nr.at[3 + h])
     ahead, other = split(ffn(1 - odd))
     rso[1] = other.astype(BF16)
     start(rso.at[1], rsi.at[1], fs.at[1], fr.at[1], sib)
+    kept, other = split(ffn(odd))
+    rso[0] = other.astype(BF16)
+    start(rso.at[0], rsi.at[0], fs.at[0], fr.at[0], sib)
     arrived(rsi.at[1], fr.at[1])
     pxo[...] = (ahead + rsi[1].astype(F32)).astype(BF16)
     start(pxo, pxi, fs.at[2], fr.at[2], pair)
@@ -596,8 +600,8 @@
 
     def sent_heads(o, carry):
         b = rem(q4 + o, 4)
-        slot = rem(q4 - b + 4, 4)
-        remote(ab.at[b], ar.at[slot], aas.at[b], aar.at[slot], (t, 4 * b + gi)).wait_send()
+        slot, dev = holder(b)
+        remote(ab.at[b], ar.at[slot], aas.at[b], aar.at[slot], dev).wait_send()
         return carry
 
     lax.fori_loop(1, 4, sent_heads, 0)
@@ -630,7 +634,7 @@
             V((NPIECE, 8, 128), F32), V((NPIECE, 8, 128), F32), V((NPIECE, 8, 128), F32), V((48, 128), F32),
             V((NK, 16, 128), BF16), V((NK, 8, 128), F32), V((NK, 16, 128), BF16), V((NK, 8, 128), F32),
             dma((16,)),
-            dma((16,)), dma((16,)), dma((17,)), dma((17,)),
+            dma((8,)), dma((8,)), dma((9,)), dma((9,)),
             dma((9,)), dma((9,)), dma((3,)), dma((3,)), dma((8,)), dma((8,)),
             dma((8,)), dma((8,)), dma((4,)), dma((4,)), dma((8,)), dma((8,)), dma((4,)), dma((4,)), dma((3,)), dma((3,)),
             dma((2,)), dma((2,)),

time: 82.1 us -> 81.1 us (0.988)
  Pallas kernels: 78.4 us -> 77.4 us
    pallas_call x1, Pallas kernels: 78.4 us -> 77.4 us  [body(): pl.pallas_call(kernel, out_shape=(jax.ShapeDtypeStruct((64, D), BF16), ja...]
where the time goes in v3:
time: 81.1 us; the launch traced here: 80.9 us
  Pallas kernels  77.4 us (95%)
  local copies, waits for them, and re-layouts  2.85 us (4%)
    pallas_call x1, Pallas kernels, body(): pl.pallas_call(kernel, out_shape=(jax.ShapeDtypeStruct((64, D), BF16), ja...  77.4 us
    unnamed x2, local copies, waits for them, and re-layouts  2.85 us

profile of v3, /device:TPU:1, one launch (start us, length us, event | category | flops | bytes accessed | tf_op | source)
XLA Modules:
  0.0 80.9 jit_solution(8894933938268122407)
XLA Ops:
  0.6 77.4 %shard_map.149 = (bf16[64,1024]{1,0:T(8,128)(2,1)}, bf16[2,1024]{1,0:T(2,128)(2,1)}) custom-call(bf16[64,1024]{1,0:T(8,128)(2,1)} %hid.1, bf16[3,64,1024]{2,1,0:T(8,128)(2,1)} %bitcast.5, s32[48]{0:T(128)} %slen_in.1, bf16[64,1024]{1,0:T(8,128)(2,1)} %wo.1, f32[1,1024]{1,0:T(1,128)} %bitcast.6, f32[1,1024]{1,0:T(1,128)} %bitcast.7, bf16[1024,256]{1,0:T(8,128)(2,1)} %up.1, ...), custom_call_target="tpu_custom_call" | custom-call | tf_op jit(solution)/shard_map/pallas_call | solution.py:616
  78.1 1.6 %copy.18 = bf16[64,1024]{1,0:T(8,128)(2,1)} copy(bf16[64,1024]{1,0:T(8,128)(2,1)} %get-tuple-element.4) | data formatting | bytes 262144
  79.6 1.3 %copy.19 = bf16[2,1024]{1,0:T(2,128)(2,1)} copy(bf16[2,1024]{1,0:T(2,128)(2,1)} %get-tuple-element.5) | data formatting | bytes 8192
